TPU v7x, 32 devices: a whole 2x2x4 slice. The times are simulated.
32 devices in a mesh: dp: 4 (over y, core), seq: 8 (over z, x).
Axes of the slice: x: 2, y: 2, z: 4, core: 2. Of those that a mesh axis runs over, the one named last changes fastest.
Arguments:
- byte_rows: bfloat16 [8, 2048, 768], P('dp', 'seq'), may hold values from -6 to 6
- segments: int32 [8, 2048], P('dp', 'seq'), may hold values from 0 to 2048, as said below
- counts: int32 [8], P('dp'), may hold values from 1024 to 2048
- buckets: int32 [2047], replicated, may hold values from 0 to 31
- cotangent: bfloat16 [8, 1024, 768], P('dp', 'seq'), may hold values from -6 to 6
- vectors: float32 [7, 768], replicated, as said below
- vector_momenta: float32 [7, 768], replicated, may hold values from -160 to 160
- bias_table: float32 [32, 12], replicated, may hold values from -4 to 4
- table_momenta: float32 [32, 12], replicated, may hold values from -56 to 56
- attention_weights: float32 [4, 768, 768], P(None, ('dp', 'seq')), as said below
- attention_left: float32 [4, 768, 768], P(None, ('dp', 'seq')), as said below
- attention_right: float32 [4, 768, 768], P(None, ('dp', 'seq')), as said below
- attention_left_root: float32 [4, 768, 768], P(None, ('dp', 'seq')), as said below
- attention_right_root: float32 [4, 768, 768], P(None, ('dp', 'seq')), as said below
- attention_momenta: float32 [4, 768, 768], P(None, ('dp', 'seq')), may hold values from -160 to 160
- expand_weights: float32 [2, 768, 2048], P(None, ('dp', 'seq')), may hold values from -0.21875 to 0.21875
- expand_left: float32 [2, 768, 768], P(None, ('dp', 'seq')), as said below
- expand_right: float32 [2, 2048, 2048], P(None, ('dp', 'seq')), as said below
- expand_left_root: float32 [2, 768, 768], P(None, ('dp', 'seq')), as said below
- expand_right_root: float32 [2, 2048, 2048], P(None, ('dp', 'seq')), as said below
- expand_momenta: float32 [2, 768, 2048], P(None, ('dp', 'seq')), may hold values from -160 to 160
- shrink_weights: float32 [2048, 768], P(('dp', 'seq')), may hold values from -0.125 to 0.125
- down_left_statistics: float32 [2048, 2048], P(('dp', 'seq')), as said below
- shrink_right: float32 [768, 768], P(('dp', 'seq')), as said below
- shrink_left_root: float32 [2048, 2048], P(('dp', 'seq')), as said below
- shrink_right_root: float32 [768, 768], P(('dp', 'seq')), as said below
- shrink_momenta: float32 [2048, 768], P(('dp', 'seq')), may hold values from -160 to 160
Outputs:
- layer_output: bfloat16 [8, 1024, 768], P('dp', 'seq')
- input_grads: float32 [8, 2048, 768], P('dp', 'seq')
- vectors_new: float32 [7, 768], replicated
- vector_momenta_new: float32 [7, 768], replicated
- table_new: float32 [32, 12], replicated
- table_momenta_new: float32 [32, 12], replicated
- attention_new: float32 [4, 768, 768], P(None, ('dp', 'seq'))
- attention_left_new: float32 [4, 768, 768], P(None, ('dp', 'seq'))
- attention_right_new: float32 [4, 768, 768], P(None, ('dp', 'seq'))
- attention_momenta_new: float32 [4, 768, 768], P(None, ('dp', 'seq'))
- attention_copy: bfloat16 [4, 768, 768], P(None, ('dp', 'seq'))
- expand_new: float32 [2, 768, 2048], P(None, ('dp', 'seq'))
- expand_left_new: float32 [2, 768, 768], P(None, ('dp', 'seq'))
- expand_right_new: float32 [2, 2048, 2048], P(None, ('dp', 'seq'))
- expand_momenta_new: float32 [2, 768, 2048], P(None, ('dp', 'seq'))
- expand_copy: bfloat16 [2, 768, 2048], P(None, ('dp', 'seq'))
- shrink_new: float32 [2048, 768], P(('dp', 'seq'))
- shrink_left_new: float32 [2048, 2048], P(('dp', 'seq'))
- shrink_right_new: float32 [768, 768], P(('dp', 'seq'))
- shrink_momenta_new: float32 [2048, 768], P(('dp', 'seq'))
- shrink_copy: bfloat16 [2048, 768], P(('dp', 'seq'))
Inputs may be any that keep to these rules, and one draw needn't show every extreme that they name: `segments`: along a row the item number never falls within its first counts bytes; bytes at or past the row's count carry 2048; in each aligned group of 2 rows one row is a single item 0 with count 2048. `vectors`: rows 0 to 3 are the causal convolution's taps, row 4 the block-score vector, rows 5 and 6 the gains of the two norms. `attention_weights`: slices 0 to 3 are the query, key, value and output projections. `attention_left`: each slice symmetric. `attention_right`: each slice symmetric. `attention_left_root`: each slice symmetric. `attention_right_root`: each slice symmetric. `expand_left`: each slice symmetric. `expand_right`: each slice symmetric. `expand_left_root`: each slice symmetric. `expand_right_root`: each slice symmetric. `down_left_statistics`: symmetric. `shrink_right`: symmetric. `shrink_left_root`: symmetric. `shrink_right_root`: symmetric.
All inputs are finite; a program needn't handle non-finite values.
Results may differ from a plain program's by a relative error of at most 0.019.
Values may be sent and summed in bfloat16 or wider, within the bound.
No kernel may reach another device: no remote copies, remote signals or barrier semaphores. Data moves between devices by JAX's collectives and lax.ppermute only.
A program may use at most 192 MiB of HBM per device.

v0:
```python
from functools import partial
import math

import jax
import jax.numpy as jnp
from jax import lax
from jax.sharding import PartitionSpec as P

EPSILON = 1e-06
STAT_DECAY = 0.95
MOMENTUM = 0.9
MATRIX_RATE = 0.1
SMALL_RATE = 0.1
MASKED = -1e30
HIGH_PRECISION = lax.Precision.HIGHEST


def padded_2(block, sides, width):
    for axis, dim in sides:
        count = lax.axis_size(axis)
        forward = [(i, i + 1) for i in range(count - 1)]
        backward = [(target, source) for source, target in forward]
        low = lax.ppermute(
            lax.slice_in_dim(block, block.shape[dim] - width, None, axis=dim), axis, forward
        )
        high = lax.ppermute(lax.slice_in_dim(block, 0, width, axis=dim), axis, backward)
        block = jnp.concatenate([low, block, high], axis=dim)
    return block


def rms_factor(values):
    return lax.rsqrt(jnp.mean(values * values, axis=-1, keepdims=True) + EPSILON)


def norm_back(values, factor, gain_row, grad_out):
    scaled = grad_out * gain_row
    grad_gain = jnp.sum(grad_out * values * factor, axis=0)
    inner_mean = jnp.mean(scaled * values, axis=-1, keepdims=True)
    return (factor * (scaled - values * inner_mean * factor * factor), grad_gain)


def block_pool(around, positions, block_size, row_total):
    length = positions.shape[0]
    summed = jnp.zeros(around.shape[:-2] + (length, around.shape[-1]), jnp.float32)
    counted = jnp.zeros((length,), jnp.float32)
    for offset in range(1 - block_size, block_size):
        nearby = positions + offset
        inside = (
            (nearby // block_size == positions // block_size) & (nearby >= 0) & (nearby < row_total)
        )
        weight = inside.astype(jnp.float32)
        summed = summed + weight[:, None] * around[..., 3 + offset : 3 + offset + length, :]
        counted = counted + weight
    return (summed, counted)


def by_blocks(step_fn, folded, pieces):
    length = pieces[0].shape[0]
    block_span = 512
    stacked = tuple(
        (
            piece_item.reshape((length // block_span, block_span) + piece_item.shape[1:])
            for piece_item in pieces
        )
    )
    offsets = block_span * jnp.arange(length // block_span, dtype=jnp.int32)

    def visit_block(inner_state, block_item):
        return (step_fn(inner_state, block_item[0], block_item[1]), None)

    result, unused = lax.scan(visit_block, folded, (stacked, offsets))
    return result


def window_base(bias_rel, query_start, query_count, key_start):
    return key_start - query_start + bias_rel.shape[0] // 2 - (query_count - 1)


def bias_window(bias_rel, query_start, query_count, key_start, key_count):
    span = query_count + key_count
    head_count = bias_rel.shape[1]
    base = window_base(bias_rel, query_start, query_count, key_start)
    window = lax.dynamic_slice_in_dim(bias_rel, base, span - 1, 0)
    padded = jnp.pad(jnp.transpose(window), ((0, 0), (0, 1)))
    rolled = jnp.roll(padded, 1 - query_count, axis=1)
    tiled = jnp.broadcast_to(rolled[:, None, :], (head_count, query_count, span))
    tiled = tiled.reshape(head_count, query_count * span)[:, : query_count * (span - 1)]
    return tiled.reshape(head_count, query_count, span - 1)[:, :, :key_count]


def bias_window_back(grad_bias, grad_scores, query_start, key_start):
    head_count, query_count, key_count = grad_scores.shape
    span = query_count + key_count
    base = window_base(grad_bias, query_start, query_count, key_start)
    spread_out = jnp.pad(grad_scores, ((0, 0), (0, 0), (0, query_count - 1)))
    flattened = jnp.pad(
        spread_out.reshape(head_count, query_count * (span - 1)), ((0, 0), (0, query_count))
    )
    column_sums = jnp.sum(flattened.reshape(head_count, query_count, span), axis=1)
    window_grad = jnp.transpose(jnp.roll(column_sums, query_count - 1, axis=1)[:, : span - 1])
    previous = lax.dynamic_slice_in_dim(grad_bias, base, span - 1, 0)
    return lax.dynamic_update_slice_in_dim(grad_bias, previous + window_grad, base, 0)


def pair_scores(query_heads, query_start, query_seg, key_heads, key_start, key_seg, bias_rel):
    raw_scores = jnp.einsum(
        "ihd,jhd->hij", query_heads, key_heads, preferred_element_type=jnp.float32
    )
    bias_block = bias_window(
        bias_rel, query_start, query_heads.shape[0], key_start, key_heads.shape[0]
    )
    same_segment = query_seg[:, None] == key_seg[None, :]
    return jnp.where(same_segment[None], raw_scores + bias_block, MASKED)


def block_scores(context, key_piece, begin_row):
    query_heads, query_start, query_seg, seg_row, bias_rel = context
    key_count = key_piece.shape[0]
    key_heads = key_piece.reshape(key_count, query_heads.shape[1], query_heads.shape[2])
    key_seg = lax.dynamic_slice_in_dim(seg_row, begin_row, key_count, 0)
    scores = pair_scores(
        query_heads, query_start, query_seg, key_heads, begin_row, key_seg, bias_rel
    )
    return (scores, key_heads)


def total_block(context, folded, pieces, begin_row):
    scores, key_heads = block_scores(context, pieces[0], begin_row)
    running_top = jnp.maximum(folded[0], jnp.max(scores, axis=-1))
    running_sum = folded[1] * jnp.exp(folded[0] - running_top) + jnp.sum(
        jnp.exp(scores - running_top[:, :, None]), axis=-1
    )
    return (running_top, running_sum)


def value_block(context, log_total, folded, pieces, begin_row):
    scores, key_heads = block_scores(context, pieces[0], begin_row)
    prob_block = jnp.exp(scores - log_total[:, :, None]).astype(jnp.bfloat16)
    value_heads = pieces[1].reshape(key_heads.shape)
    return folded + jnp.einsum(
        "hij,jhd->ihd", prob_block, value_heads, preferred_element_type=jnp.float32
    )


def back_block(context, log_total, delta_rows, grad_heads, with_keys, folded, pieces, begin_row):
    query_heads = context[0]
    query_start = context[1]
    scores, key_heads = block_scores(context, pieces[0], begin_row)
    key_count = key_heads.shape[0]
    value_heads = pieces[1].reshape(key_heads.shape)
    prob_block = jnp.exp(scores - log_total[:, :, None])
    grad_probs = jnp.einsum(
        "ihd,jhd->hij", grad_heads, value_heads, preferred_element_type=jnp.float32
    )
    grad_scores = (prob_block * (grad_probs - delta_rows[:, :, None])).astype(jnp.bfloat16)
    grad_query = folded[0] + jnp.einsum(
        "hij,jhd->ihd", grad_scores, key_heads, preferred_element_type=jnp.float32
    )
    key_grad = jnp.einsum(
        "hij,ihd->jhd", grad_scores, query_heads, preferred_element_type=jnp.float32
    ).reshape(key_count, -1)
    value_grad = jnp.einsum(
        "hij,ihd->jhd",
        prob_block.astype(jnp.bfloat16),
        grad_heads,
        preferred_element_type=jnp.float32,
    ).reshape(key_count, -1)
    grad_keys = lax.dynamic_update_slice_in_dim(folded[1], key_grad, begin_row, 0)
    grad_values = lax.dynamic_update_slice_in_dim(folded[2], value_grad, begin_row, 0)
    grad_bias = bias_window_back(folded[3], grad_scores.astype(jnp.float32), query_start, begin_row)
    return (grad_query, grad_keys, grad_values, grad_bias)


def refresh(
    rows_grad, complete_gradient, complete_momentum, left, right, right_inverse_root, owner_rank
):
    new_left = STAT_DECAY * left + (1.0 - STAT_DECAY) * jnp.einsum(
        "gmn,gkn->gmk", rows_grad, complete_gradient, precision=HIGH_PRECISION
    )
    block_span = right.shape[1]
    column_indices = lax.dynamic_slice_in_dim(
        complete_gradient, owner_rank * block_span, block_span, 2
    )
    new_right = STAT_DECAY * right + (1.0 - STAT_DECAY) * jnp.einsum(
        "ytv,ytw->yvw", column_indices, complete_gradient, precision=HIGH_PRECISION
    )
    product_columns = jnp.einsum(
        "pyk,psk->pys", complete_momentum, right_inverse_root, precision=HIGH_PRECISION
    )
    return (new_left, new_right, product_columns)


def matmul(left_side, right_side):
    return jnp.dot(left_side, right_side, preferred_element_type=jnp.float32)


def per_device(
    byte_rows,
    segments,
    counts,
    buckets,
    cotangent,
    vectors,
    vector_momenta,
    bias_table,
    table_momenta,
    attention_weights,
    attention_left,
    attention_right,
    attention_left_root,
    attention_right_root,
    attention_momenta,
    expand_weights,
    expand_left,
    expand_right,
    expand_left_root,
    expand_right_root,
    expand_momenta,
    shrink_weights,
    down_left_statistics,
    shrink_right,
    shrink_left_root,
    shrink_right_root,
    shrink_momenta,
):
    attention_full, expand_full, shrink_full = (
        lax.all_gather(attention_weights.astype(jnp.bfloat16), ("dp", "seq"), axis=1, tiled=True),
        lax.all_gather(expand_weights.astype(jnp.bfloat16), ("dp", "seq"), axis=1, tiled=True),
        lax.all_gather(shrink_weights.astype(jnp.bfloat16), ("dp", "seq"), axis=0, tiled=True),
    )
    micro_rows, width_bytes, model_width = byte_rows.shape
    seq_size = lax.axis_size("seq")
    sequence_position = lax.axis_index("seq")
    row_len = width_bytes * seq_size
    tok_local = width_bytes // 2
    tok_row = row_len // 2
    head_count = bias_table.shape[1]
    head_dim = model_width // head_count
    positions = sequence_position * width_bytes + jnp.arange(width_bytes, dtype=jnp.int32)
    is_valid = positions[None, :] < counts[:, None]
    embedded = jnp.where(is_valid[:, :, None], byte_rows, jnp.zeros_like(byte_rows))
    widened = padded_2(embedded, (("seq", 1),), 6).astype(jnp.float32)
    conv_out = sum(
        (
            vectors[tap_index] * widened[:, tap_index : tap_index + width_bytes + 9]
            for tap_index in range(4)
        )
    )
    pooled = []
    for block_size in range(1, 5):
        summed, counted = block_pool(conv_out, positions, block_size, row_len)
        pooled.append(summed / counted[:, None])
    size_scores = jnp.stack([jnp.sum(pooled_item * vectors[4], axis=-1) for pooled_item in pooled])
    size_weights = jax.nn.softmax(size_scores, axis=0)
    blended = sum(
        (size_weights[size_index][:, :, None] * pooled[size_index] for size_index in range(4))
    )
    tokens = blended.reshape(micro_rows * tok_local, 2, model_width).mean(axis=1)
    factor_one = rms_factor(tokens)
    normed = (tokens * factor_one * vectors[5]).astype(jnp.bfloat16)
    queries = matmul(normed, attention_full[0]).astype(jnp.bfloat16)
    keys_all = matmul(normed, attention_full[1]).astype(jnp.bfloat16)
    values_all = matmul(normed, attention_full[2]).astype(jnp.bfloat16)
    token_segs = segments[:, 0::2]
    seg_rows = lax.all_gather(token_segs, "seq", axis=1, tiled=True)
    onehot = (buckets[:, None] == jnp.arange(bias_table.shape[0], dtype=jnp.int32)[None, :]).astype(
        jnp.float32
    )
    bias_rel = jnp.dot(
        onehot, bias_table, precision=HIGH_PRECISION, preferred_element_type=jnp.float32
    )
    query_start = sequence_position * tok_local
    contexts = []
    log_totals = []
    outputs_f32 = []
    for row_index in range(micro_rows):
        row_lower = row_index * tok_local
        query_heads = queries[row_lower : row_lower + tok_local].reshape(
            tok_local, head_count, head_dim
        )
        key_row = keys_all[row_lower : row_lower + tok_local]
        value_row = values_all[row_lower : row_lower + tok_local]
        context = (query_heads, query_start, token_segs[row_index], seg_rows[row_index], bias_rel)
        stats_init = (
            jnp.full((head_count, tok_local), MASKED, jnp.float32),
            jnp.zeros((head_count, tok_local), jnp.float32),
        )
        value_init = jnp.zeros((tok_local, head_count, head_dim), jnp.float32)
        running_top, running_sum = by_blocks(
            partial(total_block, context),
            stats_init,
            (lax.all_gather(key_row, "seq", axis=0, tiled=True),),
        )
        log_total = running_top + jnp.log(running_sum)
        attended_row = by_blocks(
            partial(value_block, context, log_total),
            value_init,
            (
                lax.all_gather(key_row, "seq", axis=0, tiled=True),
                lax.all_gather(value_row, "seq", axis=0, tiled=True),
            ),
        )
        contexts.append(context)
        log_totals.append(log_total)
        outputs_f32.append(attended_row)
    attended = jnp.concatenate(
        [row_item.reshape(tok_local, model_width) for row_item in outputs_f32], axis=0
    ).astype(jnp.bfloat16)
    resid = tokens + matmul(attended, attention_full[3])
    factor_two = rms_factor(resid)
    normed_two = (resid * factor_two * vectors[6]).astype(jnp.bfloat16)
    gate_pre = matmul(normed_two, expand_full[0])
    upward = matmul(normed_two, expand_full[1])
    activated, gelu_back = jax.vjp(partial(jax.nn.gelu, approximate=True), gate_pre)
    hidden = (activated * upward).astype(jnp.bfloat16)
    layer_output = (
        (resid + matmul(hidden, shrink_full))
        .astype(jnp.bfloat16)
        .reshape(micro_rows, tok_local, model_width)
    )
    grad_rows_out = cotangent.reshape(-1, model_width)
    grad_shrink = jnp.einsum("tf,td->fd", hidden, grad_rows_out, preferred_element_type=jnp.float32)
    grad_hidden = jnp.einsum(
        "td,fd->tf", grad_rows_out, shrink_full, preferred_element_type=jnp.float32
    )
    grad_gate_pre = gelu_back(grad_hidden * upward)[0].astype(jnp.bfloat16)
    grad_upward = (grad_hidden * activated).astype(jnp.bfloat16)
    grad_gate_w = jnp.einsum(
        "tc,tf->cf", normed_two, grad_gate_pre, preferred_element_type=jnp.float32
    )
    grad_up_w = jnp.einsum("tc,tf->cf", normed_two, grad_upward, preferred_element_type=jnp.float32)
    grad_normed_two = jnp.einsum(
        "tf,cf->tc", grad_gate_pre, expand_full[0], preferred_element_type=jnp.float32
    ) + jnp.einsum("tf,cf->tc", grad_upward, expand_full[1], preferred_element_type=jnp.float32)
    grad_resid_norm, grad_gain_two = norm_back(resid, factor_two, vectors[6], grad_normed_two)
    grad_resid = grad_rows_out.astype(jnp.float32) + grad_resid_norm
    grad_branch = grad_resid.astype(jnp.bfloat16)
    grad_output_proj = jnp.einsum(
        "tc,td->cd", attended, grad_branch, preferred_element_type=jnp.float32
    )
    grad_attended = jnp.einsum(
        "td,cd->tc", grad_branch, attention_full[3], preferred_element_type=jnp.float32
    ).astype(jnp.bfloat16)
    grad_bias_rel = jnp.zeros_like(bias_rel)
    query_grads = []
    key_grads = []
    value_grads = []
    for row_index in range(micro_rows):
        row_lower = row_index * tok_local
        grad_heads = grad_attended[row_lower : row_lower + tok_local].reshape(
            tok_local, head_count, head_dim
        )
        delta_rows = jnp.transpose(
            jnp.sum(grad_heads.astype(jnp.float32) * outputs_f32[row_index], axis=-1)
        )
        back_init = (
            jnp.zeros((tok_local, head_count, head_dim), jnp.float32),
            jnp.zeros((tok_row, model_width), jnp.float32),
            jnp.zeros((tok_row, model_width), jnp.float32),
            jnp.zeros_like(bias_rel),
        )
        back_step = partial(
            back_block, contexts[row_index], log_totals[row_index], delta_rows, grad_heads, True
        )
        key_row = keys_all[row_lower : row_lower + tok_local]
        value_row = values_all[row_lower : row_lower + tok_local]
        folded = by_blocks(
            back_step,
            back_init,
            (
                lax.all_gather(key_row, "seq", axis=0, tiled=True),
                lax.all_gather(value_row, "seq", axis=0, tiled=True),
            ),
        )
        key_mine, value_mine = (
            lax.psum_scatter(
                folded[1].astype(jnp.bfloat16), "seq", scatter_dimension=0, tiled=True
            ).astype(jnp.float32),
            lax.psum_scatter(
                folded[2].astype(jnp.bfloat16), "seq", scatter_dimension=0, tiled=True
            ).astype(jnp.float32),
        )
        grad_bias_rel = grad_bias_rel + folded[3]
        query_grads.append(folded[0].reshape(tok_local, model_width))
        key_grads.append(key_mine)
        value_grads.append(value_mine)
    grad_query = jnp.concatenate(query_grads, axis=0).astype(jnp.bfloat16)
    grad_key = jnp.concatenate(key_grads, axis=0).astype(jnp.bfloat16)
    grad_value = jnp.concatenate(value_grads, axis=0).astype(jnp.bfloat16)
    grad_wq = jnp.einsum("tc,td->cd", normed, grad_query, preferred_element_type=jnp.float32)
    grad_wk = jnp.einsum("tc,td->cd", normed, grad_key, preferred_element_type=jnp.float32)
    grad_wv = jnp.einsum("tc,td->cd", normed, grad_value, preferred_element_type=jnp.float32)
    grad_normed = (
        jnp.einsum("td,cd->tc", grad_query, attention_full[0], preferred_element_type=jnp.float32)
        + jnp.einsum("td,cd->tc", grad_key, attention_full[1], preferred_element_type=jnp.float32)
        + jnp.einsum("td,cd->tc", grad_value, attention_full[2], preferred_element_type=jnp.float32)
    )
    grad_tokens_norm, grad_gain_one = norm_back(tokens, factor_one, vectors[5], grad_normed)
    grad_tokens = (grad_resid + grad_tokens_norm).reshape(micro_rows, tok_local, model_width)
    grad_blend = jnp.repeat(grad_tokens, 2, axis=1) * 0.5
    grad_weights = jnp.stack([jnp.sum(grad_blend * pooled_item, axis=-1) for pooled_item in pooled])
    grad_sizes = size_weights * (
        grad_weights - jnp.sum(size_weights * grad_weights, axis=0, keepdims=True)
    )
    grad_score = sum(
        (
            jnp.sum(grad_sizes[size_index][:, :, None] * pooled[size_index], axis=(0, 1))
            for size_index in range(4)
        )
    )
    grad_pooled = jnp.stack(
        [
            size_weights[size_index][:, :, None] * grad_blend
            + grad_sizes[size_index][:, :, None] * vectors[4]
            for size_index in range(4)
        ]
    )
    wide_grads = padded_2(grad_pooled.astype(jnp.bfloat16), (("seq", 2),), 6).astype(
        grad_pooled.dtype
    )
    ext_positions = sequence_position * width_bytes + jnp.arange(width_bytes + 3, dtype=jnp.int32)
    in_range = (ext_positions < row_len).astype(jnp.float32)[:, None]
    grad_conv = jnp.zeros((micro_rows, width_bytes + 3, model_width), jnp.float32)
    for block_size in range(1, 5):
        summed, counted = block_pool(
            wide_grads[block_size - 1][:, 3:], ext_positions, block_size, row_len
        )
        grad_conv = grad_conv + summed / jnp.maximum(counted, 1.0)[:, None] * in_range
    grad_embedded = sum(
        (
            vectors[tap_index] * grad_conv[:, 3 - tap_index : 3 - tap_index + width_bytes]
            for tap_index in range(4)
        )
    )
    grad_taps = [
        jnp.sum(
            grad_conv[:, :width_bytes] * widened[:, 3 + tap_index : 3 + tap_index + width_bytes],
            axis=(0, 1),
        )
        for tap_index in range(4)
    ]
    input_grads = jnp.where(is_valid[:, :, None], grad_embedded, 0.0)
    grad_vectors = jnp.stack(grad_taps + [grad_score, grad_gain_one, grad_gain_two])
    grad_table = jnp.dot(
        onehot.T, grad_bias_rel, precision=HIGH_PRECISION, preferred_element_type=jnp.float32
    )
    rows_attention, rows_expand, rows_shrink = (
        lax.psum_scatter(
            jnp.stack([grad_wq, grad_wk, grad_wv, grad_output_proj]),
            ("dp", "seq"),
            scatter_dimension=1,
            tiled=True,
        ),
        lax.psum_scatter(
            jnp.stack([grad_gate_w, grad_up_w]), ("dp", "seq"), scatter_dimension=1, tiled=True
        ),
        lax.psum_scatter(grad_shrink, ("dp", "seq"), scatter_dimension=0, tiled=True),
    )
    sum_vectors, sum_table = lax.psum((grad_vectors, grad_table), ("dp", "seq"))
    total_tokens = micro_rows * lax.axis_size("dp") * tok_row
    small_rate = SMALL_RATE / math.sqrt(total_tokens)
    vector_momenta_new = MOMENTUM * vector_momenta + sum_vectors
    vectors_new = vectors - small_rate * vector_momenta_new
    table_momenta_new = MOMENTUM * table_momenta + sum_table
    table_new = bias_table - small_rate * table_momenta_new
    owner_rank = lax.axis_index(("dp", "seq"))
    shrink_rows = rows_shrink[None]
    attention_mom_new = MOMENTUM * attention_momenta + rows_attention
    expand_mom_new = MOMENTUM * expand_momenta + rows_expand
    shrink_mom_new = MOMENTUM * shrink_momenta[None] + shrink_rows
    full_attention, full_expand, full_shrink, momenta_attention, momenta_expand, momenta_shrink = (
        lax.all_gather(
            rows_attention.astype(jnp.bfloat16), ("dp", "seq"), axis=1, tiled=True
        ).astype(rows_attention.dtype),
        lax.all_gather(rows_expand.astype(jnp.bfloat16), ("dp", "seq"), axis=1, tiled=True).astype(
            rows_expand.dtype
        ),
        lax.all_gather(shrink_rows.astype(jnp.bfloat16), ("dp", "seq"), axis=1, tiled=True).astype(
            shrink_rows.dtype
        ),
        lax.all_gather(
            attention_mom_new.astype(jnp.bfloat16), ("dp", "seq"), axis=1, tiled=True
        ).astype(attention_mom_new.dtype),
        lax.all_gather(
            expand_mom_new.astype(jnp.bfloat16), ("dp", "seq"), axis=1, tiled=True
        ).astype(expand_mom_new.dtype),
        lax.all_gather(
            shrink_mom_new.astype(jnp.bfloat16), ("dp", "seq"), axis=1, tiled=True
        ).astype(shrink_mom_new.dtype),
    )
    attention_stats = refresh(
        rows_attention,
        full_attention,
        momenta_attention,
        attention_left,
        attention_right,
        attention_right_root,
        owner_rank,
    )
    expand_stats = refresh(
        rows_expand,
        full_expand,
        momenta_expand,
        expand_left,
        expand_right,
        expand_right_root,
        owner_rank,
    )
    shrink_stats = refresh(
        shrink_rows,
        full_shrink,
        momenta_shrink,
        down_left_statistics[None],
        shrink_right[None],
        shrink_right_root[None],
        owner_rank,
    )
    cols_attention, cols_expand, cols_shrink = (
        lax.all_gather(
            attention_stats[2].astype(jnp.bfloat16), ("dp", "seq"), axis=2, tiled=True
        ).astype(jnp.float32),
        lax.all_gather(
            expand_stats[2].astype(jnp.bfloat16), ("dp", "seq"), axis=2, tiled=True
        ).astype(jnp.float32),
        lax.all_gather(
            shrink_stats[2].astype(jnp.bfloat16), ("dp", "seq"), axis=2, tiled=True
        ).astype(jnp.float32),
    )
    attention_new = attention_weights - MATRIX_RATE * jnp.einsum(
        "gmk,gkn->gmn", attention_left_root, cols_attention, precision=HIGH_PRECISION
    )
    expand_new = expand_weights - MATRIX_RATE * jnp.einsum(
        "gmk,gkn->gmn", expand_left_root, cols_expand, precision=HIGH_PRECISION
    )
    shrink_new = (
        shrink_weights
        - MATRIX_RATE
        * jnp.einsum("gmk,gkn->gmn", shrink_left_root[None], cols_shrink, precision=HIGH_PRECISION)[
            0
        ]
    )
    return (
        layer_output,
        input_grads,
        vectors_new,
        vector_momenta_new,
        table_new,
        table_momenta_new,
        attention_new,
        attention_stats[0],
        attention_stats[1],
        attention_mom_new,
        attention_new.astype(jnp.bfloat16),
        expand_new,
        expand_stats[0],
        expand_stats[1],
        expand_mom_new,
        expand_new.astype(jnp.bfloat16),
        shrink_new,
        shrink_stats[0][0],
        shrink_stats[1][0],
        shrink_mom_new[0],
        shrink_new.astype(jnp.bfloat16),
    )


def solution(mesh):
    placed = (
        P("dp", "seq", None),
        P("dp", "seq"),
        P("dp"),
        P(),
        P("dp", "seq", None),
        P(),
        P(),
        P(),
        P(),
        P(None, ("dp", "seq"), None),
        P(None, ("dp", "seq"), None),
        P(None, ("dp", "seq"), None),
        P(None, ("dp", "seq"), None),
        P(None, ("dp", "seq"), None),
        P(None, ("dp", "seq"), None),
        P(None, ("dp", "seq"), None),
        P(None, ("dp", "seq"), None),
        P(None, ("dp", "seq"), None),
        P(None, ("dp", "seq"), None),
        P(None, ("dp", "seq"), None),
        P(None, ("dp", "seq"), None),
        P(("dp", "seq"), None),
        P(("dp", "seq"), None),
        P(("dp", "seq"), None),
        P(("dp", "seq"), None),
        P(("dp", "seq"), None),
        P(("dp", "seq"), None),
    )
    return jax.shard_map(
        per_device,
        mesh=mesh,
        in_specs=placed,
        out_specs=(
            P("dp", "seq", None),
            P("dp", "seq", None),
            P(),
            P(),
            P(),
            P(),
            P(None, ("dp", "seq"), None),
            P(None, ("dp", "seq"), None),
            P(None, ("dp", "seq"), None),
            P(None, ("dp", "seq"), None),
            P(None, ("dp", "seq"), None),
            P(None, ("dp", "seq"), None),
            P(None, ("dp", "seq"), None),
            P(None, ("dp", "seq"), None),
            P(None, ("dp", "seq"), None),
            P(None, ("dp", "seq"), None),
            P(("dp", "seq"), None),
            P(("dp", "seq"), None),
            P(("dp", "seq"), None),
            P(("dp", "seq"), None),
            P(("dp", "seq"), None),
        ),
        check_vma=False,
    )
```

profile of v0, /device:TPU:0, one launch (start us, length us, event | category | flops | bytes accessed | tf_op | source)
XLA Modules:
  0.0 2003.3 jit_solution(5512237122918606195)
XLA Ops:
  33.4 44.7 %all-gather.20.cloned.1.call-done = bf16[4,768,768]{2,1,0:T(8,128)(2,1)} async-done(((bf16[4,24,768]{2,1,0:T(8,128)(2,1)}), bf16[4,768,768]{2,1,0:T(8,128)(2,1)}) %all-gather.20.cloned.1.call-update) | async-done | bytes 4718608 | tf_op jit(solution)/shard_map/all_gather | solution.py:227
  87.5 19.5 all_gather.59
  111.9 11.8 all-gather.26.cloned.1.call-done
  126.2 43.3 %all-gather.28.cloned.1.call-done = bf16[1024,768]{1,0:T(8,128)(2,1)} async-done(((bf16[128,768]{1,0:T(8,128)(2,1)}), bf16[1024,768]{1,0:T(8,128)(2,1)}) %all-gather.28.cloned.1.call-update) | async-done | bytes 1572880 | tf_op jit(solution)/shard_map/all_gather | solution.py:299
  171.2 68.1 %while.108 = (s32[]{:T(128)}, f32[12,128]{1,0:T(8,128)S(1)}, f32[12,128]{1,0:T(8,128)}, s32[1,128]{1,0:T(1,128)}, s32[2]{0:T(128)}, /*index=5*/s32[1024]{0:T(102...) while((s32[]{:T(128)}, f32[12,128]{1,0:T(8,128)S(1)}, ...), condition=%wide.region_16.17_spmd.clone, body=%wide.region_13.16_spmd.clone.sunk | while | flops 104676360 | bytes 64361104 | solution.py:71
  240.0 67.4 %while.109 = (s32[]{:T(128)}, f32[128,12,64]{0,2,1:T(8,128)}, bf16[2,512,768]{1,2,0:T(8,128)(2,1)}, s32[1,128]{1,0:T(1,128)}, s32[2]{0:T(128)}, /*index=5*/s32[1...) while((s32[]{:T(128)}, f32[128,12,64]{0,2,1:T(8,128)}, ...), condition=%wide.region_18.19_spmd.clone, body=%wide.region_17.18_spmd.clone.sunk | while | flops 204742160 | bytes 65024696 | solution.py:71
  313.7 68.3 %while.106 = (s32[]{:T(128)}, f32[12,128]{1,0:T(8,128)S(1)}, f32[12,128]{1,0:T(8,128)}, s32[1,128]{1,0:T(1,128)}, s32[2]{0:T(128)}, /*index=5*/s32[1024]{0:T(102...) while((s32[]{:T(128)}, f32[12,128]{1,0:T(8,128)S(1)}, ...), condition=%wide.region_10.11_spmd.clone, body=%wide.region_7.10_spmd.clone.sunk | while | flops 104676360 | bytes 64361104 | solution.py:71
  322.5 6.9 reshape.1507
  382.7 67.0 %while.107 = (s32[]{:T(128)}, f32[128,12,64]{0,2,1:T(8,128)}, bf16[2,512,768]{1,2,0:T(8,128)(2,1)}, s32[1,128]{1,0:T(1,128)}, s32[2]{0:T(128)}, /*index=5*/s32[1...) while((s32[]{:T(128)}, f32[128,12,64]{0,2,1:T(8,128)}, ...), condition=%wide.region_12.13_spmd.clone, body=%wide.region_11.12_spmd.clone.sunk | while | flops 204742160 | bytes 65024696 | solution.py:71
  483.3 132.6 %while.111 = (s32[]{:T(128)}, f32[128,12,64]{0,2,1:T(8,128)}, bf16[1024,768]{1,0:T(8,128)(2,1)}, bf16[1024,768]{1,0:T(8,128)(2,1)}, f32[2047,12]{0,1:T(8,128)}, ...) while((s32[]{:T(128)}, f32[128,12,64]{0,2,1:T(8,128)}, ...), condition=%wide.region_28.29_spmd.clone, body=%wide.region_26.28_spmd.clone.sunk | while | flops 511065056 | bytes 132913648 | solution.py:71
  621.4 145.3 %while.110 = (s32[]{:T(128)}, f32[128,12,64]{0,2,1:T(8,128)}, bf16[1024,768]{1,0:T(8,128)(2,1)}, bf16[1024,768]{1,0:T(8,128)(2,1)}, f32[2047,12]{0,1:T(8,128)}, ...) while((s32[]{:T(128)}, f32[128,12,64]{0,2,1:T(8,128)}, ...), condition=%wide.region_24.25_spmd.clone, body=%wide.region_22.24_spmd.clone.sunk | while | flops 511065056 | bytes 132913648 | solution.py:71
  644.7 6.9 reshape.1512
  778.5 52.8 %reduce-scatter.22.cloned.1.call-done = bf16[128,768]{1,0:T(8,128)(2,1)} async-done(((bf16[1024,768]{1,0:T(8,128)(2,1)}), bf16[128,768]{1,0:T(8,128)(2,1)}) %reduce-scatter.22.cloned.1.call-update) | async-done | bytes 196624
  832.4 66.0 %reduce-scatter.28.cloned.1.call-done = bf16[128,768]{1,0:T(8,128)(2,1)} async-done(((bf16[1024,768]{1,0:T(8,128)(2,1)}), bf16[128,768]{1,0:T(8,128)(2,1)}) %reduce-scatter.28.cloned.1.call-update) | async-done | bytes 196624
  899.5 66.5 %reduce-scatter.26.cloned.1.call-done = bf16[128,768]{1,0:T(8,128)(2,1)} async-done(((bf16[1024,768]{1,0:T(8,128)(2,1)}), bf16[128,768]{1,0:T(8,128)(2,1)}) %reduce-scatter.26.cloned.1.call-update) | async-done | bytes 196624
  983.2 11.8 pad_maximum_fusion.8
  995.1 89.6 %reduce-scatter.20.cloned.1.call-done = f32[64,768]{1,0:T(8,128)} async-done(((f32[2048,768]{1,0:T(8,128)}), f32[64,768]{1,0:T(8,128)}) %reduce-scatter.20.cloned.1.call-update) | async-done | bytes 196624 | tf_op jit(solution)/shard_map/reduce_scatter | solution.py:457
  1086.5 139.9 %reduce-scatter.16.cloned.1.call-done = f32[4,24,768]{2,1,0:T(8,128)} async-done(((f32[4,768,768]{2,1,0:T(8,128)}), f32[4,24,768]{2,1,0:T(8,128)}) %reduce-scatter.16.cloned.1.call-update) | async-done | bytes 294928 | tf_op jit(solution)/shard_map/reduce_scatter | solution.py:448
  1228.4 158.3 %reduce-scatter.18.cloned.1.call-done = f32[2,24,2048]{2,1,0:T(8,128)} async-done(((f32[2,768,2048]{2,1,0:T(8,128)}), f32[2,24,2048]{2,1,0:T(8,128)}) %reduce-scatter.18.cloned.1.call-update) | async-done | bytes 393232 | tf_op jit(solution)/shard_map/reduce_scatter | solution.py:454
  1389.4 59.3 %all-gather.46.cloned.1.call-done = bf16[2048,768]{1,0:T(8,128)(2,1)} async-done(((bf16[64,768]{1,0:T(8,128)(2,1)}), bf16[2048,768]{1,0:T(8,128)(2,1)}) %all-gather.46.cloned.1.call-update) | async-done | bytes 3145744 | tf_op jit(solution)/shard_map/all_gather | solution.py:487
  1455.2 60.0 %all-gather.34.cloned.1.call-done = bf16[4,768,768]{2,1,0:T(8,128)(2,1)} async-done(((bf16[4,24,768]{2,1,0:T(8,128)(2,1)}), bf16[4,768,768]{2,1,0:T(8,128)(2,1)}) %all-gather.34.cloned.1.call-update) | async-done | bytes 4718608 | tf_op jit(solution)/shard_map/all_gather | solution.py:481
  1522.5 64.8 %all-gather.40.cloned.1.call-done = bf16[2,768,2048]{2,1,0:T(8,128)(2,1)} async-done(((bf16[2,24,2048]{2,1,0:T(8,128)(2,1)}), bf16[2,768,2048]{2,1,0:T(8,128)(2,1)}) %all-gather.40.cloned.1.call-update) | async-done | bytes 6291472 | tf_op jit(solution)/shard_map/all_gather | solution.py:484
  1587.3 9.2 convolution_convert_fusion.5
  1644.7 44.0 %all-reduce.10 = (f32[7,768]{1,0:T(8,128)S(1)}, f32[32,12]{0,1:T(8,128)S(1)}) all-reduce(f32[7,768]{1,0:T(8,128)S(1)} %stack.101, f32[32,12]{0,1:T(8,128)S(1)} %copy-done.130), channel_id=1, replica_groups=mesh['dp'=4,'seq'=8] {'dp','seq'}, use_global_device_ids=true, to_apply=%region_49.50 | all-reduce | flops 5760 | bytes 46080 | tf_op jit(solution)/shard_map/psum | solution.py:459
  1697.6 13.3 all-gather.48.cloned.1.call-done
  1716.5 60.9 %all-gather.38.cloned.1.call-done = bf16[4,768,768]{2,1,0:T(8,128)(2,1)} async-done(((bf16[4,24,768]{2,1,0:T(8,128)(2,1)}), bf16[4,768,768]{2,1,0:T(8,128)(2,1)}) %all-gather.38.cloned.1.call-update) | async-done | bytes 4718608 | tf_op jit(solution)/shard_map/all_gather | solution.py:472
  1786.7 62.9 %all-gather.44.cloned.1.call-done = bf16[2,768,2048]{2,1,0:T(8,128)(2,1)} async-done(((bf16[2,24,2048]{2,1,0:T(8,128)(2,1)}), bf16[2,768,2048]{2,1,0:T(8,128)(2,1)}) %all-gather.44.cloned.1.call-update) | async-done | bytes 6291472 | tf_op jit(solution)/shard_map/all_gather | solution.py:475
  1849.6 8.6 fusion.99
  1860.6 54.8 %all-gather.36.cloned.1.call-done = bf16[4,768,768]{1,2,0:T(8,128)(2,1)} async-done(((bf16[4,768,24]{1,2,0:T(8,128)(2,1)}), bf16[4,768,768]{1,2,0:T(8,128)(2,1)}) %all-gather.36.cloned.1.call-update) | async-done | bytes 4718608 | tf_op jit(solution)/shard_map/all_gather | solution.py:519
  1915.4 7.1 fusion.237
  1922.5 65.2 %all-gather.42.cloned.1.call-done = bf16[2,768,2048]{1,2,0:T(8,128)(2,1)} async-done(((bf16[2,768,64]{1,2,0:T(8,128)(2,1)}), bf16[2,768,2048]{1,2,0:T(8,128)(2,1)}) %all-gather.42.cloned.1.call-update) | async-done | bytes 6291472 | tf_op jit(solution)/shard_map/all_gather | solution.py:522
  1987.7 8.6 fusion.238
  (792 shorter events, 704.1 us)
Async XLA Ops:
  7.2 1580.1 %copy-start = (f32[2,64,2048]{2,1,0:T(8,128)S(1)}, f32[2,64,2048]{2,1,0:T(8,128)}, u32[]{:S(2)}) copy-start(f32[2,64,2048]{2,1,0:T(8,128)} %param.58) | copy-start | bytes 3145732
  7.2 70.9 %all-gather.20.cloned.1.call-start = ((), (), s32[]{:S(2)}) async-start(), calls=%async_computation.7 | async-start | bytes 4866048 | tf_op jit(solution)/shard_map/all_gather | solution.py:227
  9.0 114.7 %all-gather.26.cloned.1.call-start = ((), (), s32[]{:S(2)}) async-start(), calls=%async_computation.10 | async-start | bytes 1769472 | tf_op jit(solution)/shard_map/all_gather | solution.py:300
  11.1 7.7 collective-permute-start.1
  12.4 7.0 collective-permute-start
  80.7 88.8 %all-gather.28.cloned.1.call-start = ((), (), s32[]{:S(2)}) async-start(), calls=%async_computation.11 | async-start | bytes 1769472 | tf_op jit(solution)/shard_map/all_gather | solution.py:299
  83.4 226.0 %all-gather.22.cloned.1.call-start = ((), (), s32[]{:S(2)}) async-start(), calls=%async_computation.8 | async-start | bytes 1769472 | tf_op jit(solution)/shard_map/all_gather | solution.py:300
  84.0 228.0 %all-gather.24.cloned.1.call-start = ((), (), s32[]{:S(2)}) async-start(), calls=%async_computation.9 | async-start | bytes 1769472 | tf_op jit(solution)/shard_map/all_gather | solution.py:299
  84.6 369.0 %all-gather.30.cloned.1.call-start = ((), (), s32[]{:S(2)}) async-start(), calls=%async_computation.12 | async-start | bytes 6488064 | tf_op jit(solution)/shard_map/all_gather | solution.py:228
  85.3 376.9 %all-gather.32.cloned.1.call-start = ((), (), s32[]{:S(2)}) async-start(), calls=%async_computation.13 | async-start | bytes 3244032 | tf_op jit(solution)/shard_map/all_gather | solution.py:229
  86.1 691.3 %reduce-scatter.24.cloned.1.call-start = ((), (), s32[]{:S(2)}) async-start(), calls=%async_computation.27 | async-start | bytes 1769472
  618.1 213.2 %reduce-scatter.22.cloned.1.call-start = ((), (), s32[]{:S(2)}) async-start(), calls=%async_computation.26 | async-start | bytes 1769472
  766.7 131.7 %reduce-scatter.28.cloned.1.call-start = ((), (), s32[]{:S(2)}) async-start(), calls=%async_computation.29 | async-start | bytes 1769472
  767.3 198.7 %reduce-scatter.26.cloned.1.call-start = ((), (), s32[]{:S(2)}) async-start(), calls=%async_computation.28 | async-start | bytes 1769472
  768.0 316.6 %reduce-scatter.20.cloned.1.call-start = ((), (), s32[]{:S(2)}) async-start(), calls=%async_computation.22 | async-start | bytes 6488064 | tf_op jit(solution)/shard_map/reduce_scatter | solution.py:457
  771.9 454.6 %reduce-scatter.16.cloned.1.call-start = ((), (), s32[]{:S(2)}) async-start(), calls=%async_computation.14 | async-start | bytes 9732096 | tf_op jit(solution)/shard_map/reduce_scatter | solution.py:448
  973.6 413.1 %reduce-scatter.18.cloned.1.call-start = ((), (), s32[]{:S(2)}) async-start(), calls=%async_computation.18 | async-start | bytes 12976128 | tf_op jit(solution)/shard_map/reduce_scatter | solution.py:454
  995.0 231.5 %copy-start.83 = (f32[4,24,768]{2,1,0:T(8,128)S(1)}, f32[4,24,768]{2,1,0:T(8,128)}, u32[]{:S(2)}) copy-start(f32[4,24,768]{2,1,0:T(8,128)} %param.53) | copy-start | bytes 884740
  995.0 391.7 %copy-start.79 = (f32[2,24,2048]{2,1,0:T(8,128)S(1)}, f32[2,24,2048]{2,1,0:T(8,128)}, u32[]{:S(2)}) copy-start(f32[2,24,2048]{2,1,0:T(8,128)} %param.59) | copy-start | bytes 1179652
  995.0 453.7 %all-gather.46.cloned.1.call-start = ((), (), s32[]{:S(2)}) async-start(), calls=%async_computation.23 | async-start | bytes 3244032 | tf_op jit(solution)/shard_map/all_gather | solution.py:487
  1086.5 362.2 %copy-start.99 = (f32[24,768]{1,0:T(8,128)S(1)}, f32[24,768]{1,0:T(8,128)}, u32[]{:S(2)}) copy-start(f32[24,768]{1,0:T(8,128)} %param.64) | copy-start | bytes 221188
  1086.5 428.7 %all-gather.34.cloned.1.call-start = ((), (), s32[]{:S(2)}) async-start(), calls=%async_computation.15 | async-start | bytes 4866048 | tf_op jit(solution)/shard_map/all_gather | solution.py:481
  1228.4 358.9 %all-gather.40.cloned.1.call-start = ((), (), s32[]{:S(2)}) async-start(), calls=%async_computation.19 | async-start | bytes 6488064 | tf_op jit(solution)/shard_map/all_gather | solution.py:484
  1388.8 301.2 %all-gather.50.cloned.1.call-start = ((), (), s32[]{:S(2)}) async-start(), calls=%async_computation.25 | async-start | bytes 3244032 | tf_op jit(solution)/shard_map/all_gather | solution.py:478
  1389.4 321.5 %all-gather.48.cloned.1.call-start = ((), (), s32[]{:S(2)}) async-start(), calls=%async_computation.24 | async-start | bytes 3244032 | tf_op jit(solution)/shard_map/all_gather | solution.py:525
  1453.8 323.6 %all-gather.38.cloned.1.call-start = ((), (), s32[]{:S(2)}) async-start(), calls=%async_computation.17 | async-start | bytes 4866048 | tf_op jit(solution)/shard_map/all_gather | solution.py:472
  1454.4 395.2 %all-gather.44.cloned.1.call-start = ((), (), s32[]{:S(2)}) async-start(), calls=%async_computation.21 | async-start | bytes 6488064 | tf_op jit(solution)/shard_map/all_gather | solution.py:475
  1455.1 460.2 %all-gather.36.cloned.1.call-start = ((), (), s32[]{:S(2)}) async-start(), calls=%async_computation.16 | async-start | bytes 4866048 | tf_op jit(solution)/shard_map/all_gather | solution.py:519
  1522.0 465.6 %all-gather.42.cloned.1.call-start = ((), (), s32[]{:S(2)}) async-start(), calls=%async_computation.20 | async-start | bytes 6488064 | tf_op jit(solution)/shard_map/all_gather | solution.py:522
  1624.7 7.2 collective-permute-start.3
  1626.3 9.6 collective-permute-start.2
  1860.6 127.1 %copy-start.94 = (f32[2,24,768]{2,1,0:T(8,128)S(1)}, f32[2,24,768]{2,1,0:T(8,128)}, u32[]{:S(2)}) copy-start(f32[2,24,768]{2,1,0:T(8,128)} %param.57) | copy-start | bytes 442372
  (147 other events, 2021.8 us)
Sparse Core Ops, SparseCore 0:
  11.7 66.3 all-gather.19
  80.9 42.7 all-gather.25
  126.4 43.0 all-gather.27
  172.1 42.9 all-gather.21
  217.8 42.8 all-gather.23
  263.9 68.4 all-gather.29
  335.9 57.5 all-gather.31
  618.2 64.2 reduce-scatter.23
  766.8 64.4 reduce-scatter.21
  834.6 63.7 reduce-scatter.27
  902.2 63.7 reduce-scatter.25
  971.5 113.1 reduce-scatter.19
  1091.6 134.8 reduce-scatter.15
  1232.4 154.3 reduce-scatter.17
  1390.5 58.1 all-gather.45
  1452.7 62.5 all-gather.33
  1518.9 68.3 all-gather.39
  1591.1 58.6 all-gather.49
  1653.8 57.1 all-gather.47
  1714.9 62.5 all-gather.37
  1781.2 68.3 all-gather.43
  1853.1 62.1 all-gather.35
  1919.2 68.4 all-gather.41
where the time goes:
time: 2020 us; the launch traced here: 2000 us
  waiting for transfers between devices  1120 us (55%)
  local copies, waits for them, and re-layouts  439 us (22%)
  matrix products  210 us (10%)
  other arithmetic  91.1 us (5%)
  blocking collectives  63.5 us (3%)
  loops' own time  46.3 us (2%)
    unnamed x27, waiting for transfers between devices  190 us
    reduce_scatter x1, waiting for transfers between devices, per_device(): lax.psum_scatter(jnp.stack([grad_gate_w, grad_up_w]), ('dp', 'seq'), scat...  158 us
    reduce_scatter x1, waiting for transfers between devices, per_device(): lax.psum_scatter(jnp.stack([grad_wq, grad_wk, grad_wv, grad_output_proj])...  140 us
    while x120, local copies, waits for them, and re-layouts  104 us
    reduce_scatter x1, waiting for transfers between devices, per_device(): lax.psum_scatter(grad_shrink, ('dp', 'seq'), scatter_dimension=0, tiled=T...  89.6 us
    reshape x12, local copies, waits for them, and re-layouts, bias_window(): return tiled.reshape(head_count, query_count, span - 1)[:, :, :key_count]  82.3 us
    all_gather x1, waiting for transfers between devices, per_device(): lax.all_gather(expand_stats[2].astype(jnp.bfloat16), ('dp', 'seq'), axis=...  65.2 us
    all_gather x1, waiting for transfers between devices, per_device(): lax.all_gather(expand_mom_new.astype(jnp.bfloat16), ('dp', 'seq'), axis=1...  64.8 us
  transfers between devices with their start and end apart: 27, of which 19 were waited for; matrix products, arithmetic and copies ran while one was open for 28% of the time, Pallas kernels for 0%

commit v1 on v0

v1 whole, which is shorter than its diff:
```python
import functools
import math

import jax
import jax.numpy as jnp
from jax import lax
from jax.experimental import pallas as pl
from jax.experimental.pallas import tpu as pltpu
from jax.sharding import PartitionSpec as P

EPSILON = 1e-06
STAT_DECAY = 0.95
MOMENTUM = 0.9
MATRIX_RATE = 0.1
SMALL_RATE = 0.1
MASKED = -1e30
HIGH_PRECISION = lax.Precision.HIGHEST
BOTH = ("dp", "seq")


def fill_bias(brel_ref, bias_sc, heads, tile):
    span = brel_ref.shape[1]
    rows = lax.broadcasted_iota(jnp.int32, (8, span), 0)
    for h in range(heads):
        wide = jnp.broadcast_to(brel_ref[h:h + 1, :], (8, span))
        first = wide
        for i in range(8):
            first = jnp.where(rows == i, pltpu.roll(wide, span - (tile - 1) + i, 1), first)
        bias_sc[h, 0:8, :] = first
        size = 8
        while size < tile:
            bias_sc[h, size:2 * size, :] = pltpu.roll(bias_sc[h, 0:size, :], size, 1)
            size *= 2

def attn_fwd_kernel(heads, tile, qkv_ref, brel_ref, segc_ref, segr_ref, out_ref, outf_ref, lse_ref, bias_sc):
    step = pl.program_id(0)
    length = qkv_ref.shape[0]
    width = qkv_ref.shape[1] // 3
    dh = width // heads

    @pl.when(step == 0)
    def _():
        fill_bias(brel_ref, bias_sc, heads, tile)

    begin = pl.multiple_of(step * tile, tile)
    offset = pl.multiple_of(length - tile - begin, 128)
    same = segc_ref[...] == segr_ref[...]
    lanes = lax.broadcasted_iota(jnp.int32, (tile, 128), 1)
    lse_all = jnp.zeros((tile, 128), jnp.float32)
    outs = []
    for h in range(heads):
        q = qkv_ref[pl.ds(begin, tile), h * dh:(h + 1) * dh]
        k = qkv_ref[:, width + h * dh:width + (h + 1) * dh]
        v = qkv_ref[:, 2 * width + h * dh:2 * width + (h + 1) * dh]
        scores = lax.dot_general(q, k, (((1,), (1,)), ((), ())), preferred_element_type=jnp.float32)
        scores = jnp.where(same, scores + bias_sc[h, :, pl.ds(offset, length)], MASKED)
        top = jnp.max(scores, axis=1, keepdims=True)
        probs = jnp.exp(scores - top)
        total = jnp.sum(probs, axis=1, keepdims=True)
        out = lax.dot_general(probs.astype(jnp.bfloat16), v, (((1,), (0,)), ((), ())), preferred_element_type=jnp.float32)
        outs.append(out / total)
        lse_all = jnp.where(lanes == h, top + jnp.log(total), lse_all)
    joined = jnp.concatenate(outs, axis=1)
    out_ref[...] = joined.astype(jnp.bfloat16)
    outf_ref[...] = joined
    lse_ref[...] = lse_all

def attn_fwd(qkv, brel, segc, segr, heads, tile=128):
    length = qkv.shape[0]; width = qkv.shape[1] // 3
    full = lambda s: pl.BlockSpec(s, lambda i: (0,) * len(s))
    rowb = lambda w: pl.BlockSpec((tile, w), lambda i: (i, 0))
    return pl.pallas_call(
        functools.partial(attn_fwd_kernel, heads, tile),
        grid=(length // tile,),
        in_specs=[full(qkv.shape), full(brel.shape), rowb(1), full(segr.shape)],
        out_specs=[rowb(width), rowb(width), rowb(128)],
        out_shape=[jax.ShapeDtypeStruct((length, width), jnp.bfloat16), jax.ShapeDtypeStruct((length, width), jnp.float32), jax.ShapeDtypeStruct((length, 128), jnp.float32)],
        scratch_shapes=[pltpu.VMEM((heads, tile, 2 * length), jnp.float32)],
        compiler_params=pltpu.CompilerParams(vmem_limit_bytes=48 * 2**20),
        cost_estimate=pl.CostEstimate(flops=4 * length * length * width, bytes_accessed=6 * length * width * 2, transcendentals=heads * length * length),
    )(qkv, brel, segc, segr)

def attn_bwd_kernel(heads, tile, trans, qkv_ref, grad_ref, outf_ref, lse_ref, brel_ref, segc_ref, segr_ref, dqkv_ref, gb_ref, bias_sc, gb_sc, dk_sc, dv_sc):
    step = pl.program_id(0)
    length = qkv_ref.shape[0]
    width = qkv_ref.shape[1] // 3
    dh = width // heads

    @pl.when(step == 0)
    def _():
        fill_bias(brel_ref, bias_sc, heads, tile)
        gb_sc[...] = jnp.zeros_like(gb_sc)
        dk_sc[...] = jnp.zeros_like(dk_sc)
        dv_sc[...] = jnp.zeros_like(dv_sc)

    begin = pl.multiple_of(step * tile, tile)
    offset = pl.multiple_of(length - tile - begin, 128)
    same = segc_ref[...] == segr_ref[...]
    dqs = []
    for h in range(heads):
        q = qkv_ref[pl.ds(begin, tile), h * dh:(h + 1) * dh]
        k = qkv_ref[:, width + h * dh:width + (h + 1) * dh]
        v = qkv_ref[:, 2 * width + h * dh:2 * width + (h + 1) * dh]
        g = grad_ref[:, h * dh:(h + 1) * dh]
        delta = jnp.sum(g.astype(jnp.float32) * outf_ref[:, h * dh:(h + 1) * dh], axis=1, keepdims=True)
        lse = lse_ref[:, h:h + 1]
        scores = lax.dot_general(q, k, (((1,), (1,)), ((), ())), preferred_element_type=jnp.float32)
        scores = jnp.where(same, scores + bias_sc[h, :, pl.ds(offset, length)], MASKED)
        probs = jnp.exp(scores - lse)
        gp = lax.dot_general(g, v, (((1,), (1,)), ((), ())), preferred_element_type=jnp.float32)
        gs = (probs * (gp - delta))
        gsb = gs.astype(jnp.bfloat16)
        pb = probs.astype(jnp.bfloat16)
        gb_sc[h, :, pl.ds(offset, length)] += gsb.astype(jnp.float32)
        dqs.append(lax.dot_general(gsb, k, (((1,), (0,)), ((), ())), preferred_element_type=jnp.float32))
        if trans:
            dk_sc[h] += lax.dot_general(q, gsb, (((0,), (0,)), ((), ())), preferred_element_type=jnp.float32)
            dv_sc[h] += lax.dot_general(g, pb, (((0,), (0,)), ((), ())), preferred_element_type=jnp.float32)
        else:
            dk_sc[h] += lax.dot_general(gsb, q, (((0,), (0,)), ((), ())), preferred_element_type=jnp.float32)
            dv_sc[h] += lax.dot_general(pb, g, (((0,), (0,)), ((), ())), preferred_element_type=jnp.float32)
    dqkv_ref[pl.ds(begin, tile), 0:width] = jnp.concatenate(dqs, axis=1).astype(jnp.bfloat16)

    @pl.when(step == pl.num_programs(0) - 1)
    def _():
        turn = (lambda x: x.T) if trans else (lambda x: x)
        dqkv_ref[:, width:3 * width] = jnp.concatenate(
            [turn(dk_sc[h]) for h in range(heads)] + [turn(dv_sc[h]) for h in range(heads)], axis=1).astype(jnp.bfloat16)
        span = gb_sc.shape[2]
        rows = lax.broadcasted_iota(jnp.int32, (8, span), 0)
        for h in range(heads):
            size = tile // 2
            part = gb_sc[h]
            while size >= 8:
                part = part[:size] + pltpu.roll(part[size:], span - size, 1)
                size //= 2
            line = jnp.zeros((1, span), jnp.float32)
            for i in range(8):
                line = line + jnp.sum(jnp.where(rows == i, pltpu.roll(part, (tile - 1 - i) % span, 1), 0.0), axis=0, keepdims=True)
            gb_ref[h:h + 1, :] = line

def attn_bwd(qkv, grad, outf, lse, brel, segc, segr, heads, tile=128, trans=True):
    length = qkv.shape[0]; width = qkv.shape[1] // 3; dh = width // heads
    full = lambda s: pl.BlockSpec(s, lambda i: (0,) * len(s))
    rowb = lambda w: pl.BlockSpec((tile, w), lambda i: (i, 0))
    acc = (heads, dh, length) if trans else (heads, length, dh)
    return pl.pallas_call(
        functools.partial(attn_bwd_kernel, heads, tile, trans),
        grid=(length // tile,),
        in_specs=[full(qkv.shape), rowb(width), rowb(width), rowb(128), full(brel.shape), rowb(1), full(segr.shape)],
        out_specs=[full(qkv.shape), full(brel.shape)],
        out_shape=[jax.ShapeDtypeStruct(qkv.shape, jnp.bfloat16), jax.ShapeDtypeStruct(brel.shape, jnp.float32)],
        scratch_shapes=[pltpu.VMEM((heads, tile, 2 * length), jnp.float32), pltpu.VMEM((heads, tile, 2 * length), jnp.float32), pltpu.VMEM(acc, jnp.float32), pltpu.VMEM(acc, jnp.float32)],
        compiler_params=pltpu.CompilerParams(vmem_limit_bytes=56 * 2**20),
        cost_estimate=pl.CostEstimate(flops=10 * length * length * width, bytes_accessed=12 * length * width * 2, transcendentals=heads * length * length),
    )(qkv, grad, outf, lse, brel, segc, segr)


def low(values):
    return values.astype(jnp.bfloat16)


def dot(left_side, right_side, left_dim, right_dim):
    return lax.dot_general(
        left_side,
        right_side,
        (((left_dim,), (right_dim,)), ((), ())),
        preferred_element_type=jnp.float32,
    )


def padded_2(block, sides, width):
    for axis, dim in sides:
        count = lax.axis_size(axis)
        forward = [(i, i + 1) for i in range(count - 1)]
        backward = [(target, source) for source, target in forward]
        low_side = lax.ppermute(
            lax.slice_in_dim(block, block.shape[dim] - width, None, axis=dim), axis, forward
        )
        high_side = lax.ppermute(lax.slice_in_dim(block, 0, width, axis=dim), axis, backward)
        block = jnp.concatenate([low_side, block, high_side], axis=dim)
    return block


def rms_factor(values):
    return lax.rsqrt(jnp.mean(values * values, axis=-1, keepdims=True) + EPSILON)


def norm_back(values, factor, gain_row, grad_out):
    scaled = grad_out * gain_row
    grad_gain = jnp.sum(grad_out * values * factor, axis=0)
    inner_mean = jnp.mean(scaled * values, axis=-1, keepdims=True)
    return (factor * (scaled - values * inner_mean * factor * factor), grad_gain)


def block_pool(around, positions, block_size, row_total):
    length = positions.shape[0]
    summed = jnp.zeros(around.shape[:-2] + (length, around.shape[-1]), jnp.float32)
    counted = jnp.zeros((length,), jnp.float32)
    for offset in range(1 - block_size, block_size):
        nearby = positions + offset
        inside = (
            (nearby // block_size == positions // block_size) & (nearby >= 0) & (nearby < row_total)
        )
        weight = inside.astype(jnp.float32)
        summed = summed + weight[:, None] * around[..., 3 + offset : 3 + offset + length, :]
        counted = counted + weight
    return (summed, counted)


class Layout:
    def __init__(self, head_count, micro_rows):
        self.dp_size = lax.axis_size("dp")
        self.seq_size = lax.axis_size("seq")
        self.count = self.dp_size * self.seq_size
        self.dp = lax.axis_index("dp")
        self.seq = lax.axis_index("seq")
        self.micro = micro_rows
        self.parts = math.gcd(self.dp_size, head_count & -head_count)
        self.groups = self.dp_size // self.parts
        self.part = self.dp % self.parts
        self.head_groups = head_count & -head_count
        self.repeat = self.seq_size // (micro_rows * self.head_groups)
        self.unit = self.seq // self.repeat
        self.matrices = 4
        self.sides = self.seq_size // self.matrices
        self.matrix = self.seq // self.sides
        self.side = self.seq % self.sides
        self.members = [
            [
                (group * self.parts + part) * self.seq_size + matrix * self.sides + side
                for part in range(self.parts)
                for side in range(self.sides)
            ]
            for group in range(self.groups)
            for matrix in range(self.matrices)
        ]
        self.holders = [
            [
                dp * self.seq_size + matrix * self.sides + side
                for dp in range(self.dp_size)
                for side in range(self.sides)
            ]
            for matrix in range(self.matrices)
        ]
        self.owners = [
            [matrix * self.sides + side for matrix in range(self.matrices)]
            for side in range(self.sides)
        ]

    def flip(self, block, axis, bits):
        size = lax.axis_size(axis)
        return lax.ppermute(block, axis, [(i, i ^ bits) for i in range(size)])

    def gather_parts(self, block):
        pieces = {0: block}
        bit = self.parts // 2
        while bit:
            for key in list(pieces):
                pieces[key | bit] = self.flip(pieces[key], "dp", bit)
            bit //= 2
        whole = jnp.zeros((self.parts,) + block.shape, block.dtype)
        for key, piece in pieces.items():
            whole = lax.dynamic_update_index_in_dim(whole, piece, self.part ^ key, 0)
        return whole

    def scatter(self, blocks, axis, index):
        bit = 1
        while blocks.shape[0] > 1:
            pairs = blocks.reshape((blocks.shape[0] // 2, 2) + blocks.shape[1:])
            mine = (index // bit) % 2
            kept = lax.dynamic_index_in_dim(pairs, mine, 1, False)
            sent = lax.dynamic_index_in_dim(pairs, 1 - mine, 1, False)
            blocks = kept.astype(jnp.float32) + self.flip(low(sent), axis, bit).astype(jnp.float32)
            bit *= 2
        return blocks[0]

    def scatter_parts(self, blocks):
        return self.scatter(blocks, "dp", self.part)

    def sum_groups(self, block):
        total = block
        for shift in range(1, self.groups):
            turn = [(i, (i + shift * self.parts) % self.dp_size) for i in range(self.dp_size)]
            total = total + lax.ppermute(low(block), "dp", turn).astype(jnp.float32)
        return total

    def sum_all(self, block):
        for axis in BOTH:
            bit = 1
            while bit < lax.axis_size(axis):
                block = block + self.flip(block, axis, bit)
                bit *= 2
        return block

    def to_units(self, blocks):
        shape = blocks.shape
        blocks = blocks[:, :, None]
        if self.repeat > 1:
            blocks = jnp.broadcast_to(blocks, shape[:2] + (self.repeat,) + shape[2:])
        return self.exchange(blocks.reshape((self.seq_size,) + shape[2:]))

    def exchange(self, blocks):
        return lax.all_to_all(blocks, "seq", 0, 0, tiled=True)

    def gather_members(self, block):
        whole = lax.all_gather(block, BOTH, axis=0, axis_index_groups=self.members)
        return whole.reshape((self.parts, self.sides) + block.shape)

    def gather_holders(self, block):
        whole = lax.all_gather(block, BOTH, axis=0, axis_index_groups=self.holders)
        return whole.reshape((self.dp_size, self.sides) + block.shape)

    def exchange_holders(self, blocks):
        return lax.all_to_all(
            blocks, BOTH, 0, 0, tiled=True, axis_index_groups=self.holders
        )

    def exchange_owners(self, blocks):
        return lax.all_to_all(
            blocks, "seq", 0, 0, tiled=True, axis_index_groups=self.owners
        )

    def block_rows(self, whole):
        span = whole.shape[0] // self.count
        view = whole.reshape((self.dp_size, self.matrices, self.sides, span) + whole.shape[1:])
        view = lax.dynamic_index_in_dim(view, self.dp, 0, False)
        return lax.dynamic_index_in_dim(view, self.side, 1, False)


def gather_all(block):
    return lax.all_gather(block, BOTH, axis=0, tiled=True)


def per_device(
    byte_rows,
    segments,
    counts,
    buckets,
    cotangent,
    vectors,
    vector_momenta,
    bias_table,
    table_momenta,
    attention_weights,
    attention_left,
    attention_right,
    attention_left_root,
    attention_right_root,
    attention_momenta,
    expand_weights,
    expand_left,
    expand_right,
    expand_left_root,
    expand_right_root,
    expand_momenta,
    shrink_weights,
    down_left_statistics,
    shrink_right,
    shrink_left_root,
    shrink_right_root,
    shrink_momenta,
):
    micro_rows, width_bytes, model_width = byte_rows.shape
    head_count = bias_table.shape[1]
    at = Layout(head_count, micro_rows)
    parts, part, seq_size, sequence_position = at.parts, at.part, at.seq_size, at.seq
    row_len = width_bytes * seq_size
    tok_local = width_bytes // 2
    tok_row = row_len // 2
    hidden_width = shrink_weights.shape[1 - 1] * at.count
    heads = head_count // parts
    head_width = model_width // parts
    hidden_part = hidden_width // parts

    row_span = model_width // at.count
    hidden_span = hidden_width // at.count
    dp_size, sides, matrices = at.dp_size, at.sides, at.matrices

    split = low(attention_weights[:3]).reshape(3, row_span, at.head_groups, head_width)
    split = jnp.transpose(split, (2, 1, 0, 3)).reshape(at.head_groups, row_span, 3 * head_width)
    split = at.to_units(jnp.broadcast_to(split[None], (micro_rows,) + split.shape))
    split = split.reshape(seq_size * row_span, 3 * head_width)
    if at.groups == 1:
        weights_qkv = at.gather_parts(split)
    else:
        weights_qkv = lax.all_gather(split, "dp", axis=0)
    weights_qkv = weights_qkv.reshape(model_width, 3 * head_width)

    rest = jnp.concatenate(
        [
            low(attention_weights[3]),
            low(expand_weights[0]),
            low(expand_weights[1]),
            low(shrink_weights).reshape(row_span, hidden_width),
        ],
        axis=1,
    )
    rest = gather_all(rest)

    def columns(whole, begin, width):
        return lax.dynamic_slice_in_dim(whole, begin, width, 1)

    weights_out = rest[:, :model_width]
    weights_expand = jnp.concatenate(
        [
            columns(rest, model_width + i * hidden_width + part * hidden_part, hidden_part)
            for i in range(2)
        ],
        axis=1,
    )
    weights_shrink = lax.dynamic_slice(
        rest,
        (part * (model_width // parts), model_width + 2 * hidden_width),
        (model_width // parts, hidden_width),
    ).reshape(hidden_part, model_width)

    grad_rows_out = cotangent.reshape(-1, model_width)
    grad_rows_all = at.gather_parts(grad_rows_out).reshape(-1, model_width)
    token_segs = segments[:, 0::2]
    seg_row = at.to_units(
        jnp.broadcast_to(token_segs[:, None], (micro_rows, at.head_groups, tok_local))
    ).reshape(tok_row)

    blank = jnp.zeros((row_span, hidden_width + model_width), jnp.bfloat16)
    side_width = (3 * model_width + hidden_width) // sides

    def early_block(i):
        if i == 2:
            feed = [low(shrink_momenta).reshape(row_span, hidden_width), low(shrink_right_root)]
        elif i < 2:
            feed = [low(expand_momenta[i]), low(expand_left_root[i])]
        else:
            feed = [blank]
        joined = jnp.concatenate(
            [low(attention_momenta[i]), low(attention_right_root[i])] + feed, axis=1
        )
        return jnp.transpose(joined.reshape(row_span, sides, side_width), (1, 0, 2))

    early = at.exchange(jnp.concatenate([early_block(i) for i in range(matrices)], axis=0))
    early = at.gather_holders(early.reshape(seq_size * row_span, side_width))
    early = early.reshape(dp_size, sides, seq_size * row_span, side_width)
    early = jnp.transpose(early, (0, 2, 1, 3)).reshape(model_width, sides * side_width)
    attention_old = early[:, :model_width]
    attention_right_whole = early[:, model_width : 2 * model_width]
    feed_old = early[:, 2 * model_width : 2 * model_width + hidden_width]
    feed_left_whole = early[:, 2 * model_width + hidden_width :]
    feed_old = jnp.where(
        at.matrix == 2, feed_old.reshape(hidden_width, model_width).T, feed_old
    )
    roots = jnp.stack(
        [low(expand_right_root[0]), low(expand_right_root[1]), low(shrink_left_root)]
        + [jnp.zeros(shrink_left_root.shape, jnp.bfloat16)]
    )
    feed_right_rows = at.exchange_owners(roots).reshape(-1, hidden_width)
    attention_left_rows = at.exchange_owners(low(attention_left_root)).reshape(-1, model_width)

    positions = sequence_position * width_bytes + jnp.arange(width_bytes, dtype=jnp.int32)
    is_valid = positions[None, :] < counts[:, None]
    embedded = jnp.where(is_valid[:, :, None], byte_rows, jnp.zeros_like(byte_rows))
    widened = padded_2(embedded, (("seq", 1),), 6).astype(jnp.float32)
    conv_out = sum(
        (
            vectors[tap_index] * widened[:, tap_index : tap_index + width_bytes + 9]
            for tap_index in range(4)
        )
    )
    pooled = []
    for block_size in range(1, 5):
        summed, counted = block_pool(conv_out, positions, block_size, row_len)
        pooled.append(summed / counted[:, None])
    size_scores = jnp.stack([jnp.sum(pooled_item * vectors[4], axis=-1) for pooled_item in pooled])
    size_weights = jax.nn.softmax(size_scores, axis=0)
    blended = sum(
        (size_weights[size_index][:, :, None] * pooled[size_index] for size_index in range(4))
    )
    tokens = blended.reshape(micro_rows * tok_local, 2, model_width).mean(axis=1)
    factor_one = rms_factor(tokens)
    normed = low(tokens * factor_one * vectors[5])

    normed_row = at.to_units(
        jnp.broadcast_to(
            normed.reshape(micro_rows, 1, tok_local, model_width),
            (micro_rows, at.head_groups, tok_local, model_width),
        )
    ).reshape(tok_row, model_width)
    qkv_row = low(dot(normed_row, weights_qkv, 1, 0))
    onehot = (buckets[:, None] == jnp.arange(bias_table.shape[0], dtype=jnp.int32)[None, :]).astype(
        jnp.float32
    )
    head_begin = (at.unit % at.head_groups) * heads
    part_table = lax.dynamic_slice_in_dim(bias_table, head_begin, heads, 1)
    bias_rel = jnp.einsum("xb,bh->hx", onehot, part_table, precision=HIGH_PRECISION)
    bias_rel = jnp.pad(bias_rel, ((0, 0), (0, 1)))
    seg_col = seg_row[:, None]
    seg_line = seg_row[None, :]
    tile = min(256, tok_row)
    attended_row, attended_f32, log_totals = attn_fwd(
        qkv_row, bias_rel, seg_col, seg_line, heads, tile
    )

    attended = at.exchange(attended_row.reshape(seq_size, tok_local, head_width))
    attended = attended.reshape(
        micro_rows, at.head_groups, at.repeat, tok_local, head_width
    )[:, :, 0]
    attended = jnp.transpose(attended, (0, 2, 1, 3)).reshape(-1, model_width)
    resid = tokens + dot(attended, weights_out, 1, 0)
    factor_two = rms_factor(resid)
    normed_two = low(resid * factor_two * vectors[6])

    normed_two_all = at.gather_parts(normed_two).reshape(-1, model_width)
    expanded = dot(normed_two_all, weights_expand, 1, 0)
    gate_pre = expanded[:, :hidden_part]
    upward = expanded[:, hidden_part:]
    activated, gelu_back = jax.vjp(functools.partial(jax.nn.gelu, approximate=True), gate_pre)
    hidden = low(activated * upward)
    grad_hidden = dot(grad_rows_all, weights_shrink, 1, 1)
    grad_gate_pre = low(gelu_back(grad_hidden * upward)[0])
    grad_upward = low(grad_hidden * activated)
    grad_expanded = jnp.concatenate([grad_gate_pre, grad_upward], axis=1)
    grad_normed_two = at.scatter_parts(
        dot(grad_expanded, weights_expand, 1, 1).reshape(parts, -1, model_width)
    )
    shrink_out = at.scatter_parts(
        dot(hidden, weights_shrink, 1, 0).reshape(parts, -1, model_width)
    )
    layer_output = low(resid + shrink_out).reshape(micro_rows, tok_local, model_width)
    grad_shrink_t = dot(grad_rows_all, hidden, 0, 0)
    grad_gate_w = dot(normed_two_all, grad_gate_pre, 0, 0)
    grad_up_w = dot(normed_two_all, grad_upward, 0, 0)

    grad_resid_norm, grad_gain_two = norm_back(resid, factor_two, vectors[6], grad_normed_two)
    grad_resid = grad_rows_out.astype(jnp.float32) + grad_resid_norm
    grad_branch = low(grad_resid)
    grad_attended = low(dot(grad_branch, weights_out, 1, 1))
    grad_attended = jnp.transpose(
        grad_attended.reshape(micro_rows, tok_local, at.head_groups, 1, head_width), (0, 2, 3, 1, 4)
    )
    grad_attended = jnp.pad(
        grad_attended, ((0, 0), (0, 0), (0, at.repeat - 1), (0, 0), (0, 0))
    )
    grad_attended_row = at.exchange(
        grad_attended.reshape(seq_size, tok_local, head_width)
    ).reshape(tok_row, head_width)
    grad_output_proj = at.scatter_parts(
        dot(attended, grad_branch, 0, 0).reshape(parts, model_width // parts, model_width)
    )

    def to_sides(block):
        return block.reshape((sides, block.shape[0] // sides) + block.shape[1:])

    feed_blocks = [to_sides(low(item)) for item in (grad_gate_w, grad_up_w, grad_shrink_t)]
    out_block = to_sides(low(grad_output_proj)).reshape(sides, -1, hidden_part)
    out_rows = out_block.shape[1]
    out_block = jnp.pad(
        out_block, ((0, 0), (0, feed_blocks[0].shape[1] - out_rows), (0, 0))
    )
    feed_sum = at.scatter(jnp.concatenate(feed_blocks + [out_block], axis=0), "seq", at.seq)
    feed_sum = at.gather_members(low(at.sum_groups(feed_sum)))
    full_output = feed_sum[:, :, :out_rows].reshape(model_width, model_width)
    full_feed = jnp.transpose(feed_sum, (1, 2, 0, 3)).reshape(model_width, hidden_width)

    def new_momenta(old, full):
        return low(MOMENTUM * old.astype(jnp.float32) + full.astype(jnp.float32))

    def strips(full):
        return at.block_rows(full).reshape(-1, full.shape[1])

    is_shrink = at.matrix == 2
    full_feed_t = full_feed.T
    feed_rows = strips(full_feed)
    feed_cols = strips(full_feed_t)
    feed_left = low(dot(feed_rows, full_feed, 1, 1))
    feed_right = low(dot(feed_cols, full_feed_t, 1, 1))
    feed_product = low(dot(new_momenta(feed_old, full_feed), feed_right_rows, 1, 1))
    feed_step = low(dot(feed_left_whole, feed_product, 1, 0))
    own_cols = feed_step.shape[1]
    moved = feed_step.reshape(dp_size, matrices, sides, row_span, own_cols)
    moved = jnp.transpose(moved, (0, 2, 1, 3, 4)).reshape(
        dp_size * sides, matrices * row_span, own_cols
    )
    moved = at.exchange_holders(moved).reshape(
        dp_size, sides, matrices * row_span, matrices, hidden_span
    )
    moved = jnp.transpose(moved, (2, 0, 3, 1, 4)).reshape(matrices, row_span, hidden_width)
    feed_step = jnp.where(
        is_shrink, feed_step.T.reshape(matrices, row_span, hidden_width), moved
    )
    feed_grad = jnp.where(
        is_shrink,
        feed_cols.reshape(matrices, row_span, hidden_width),
        feed_rows.reshape(matrices, row_span, hidden_width),
    )
    feed_out = at.exchange_owners(
        jnp.concatenate(
            [feed_step, feed_grad, feed_right.reshape(matrices, hidden_span, hidden_width)], axis=1
        )
    ).astype(jnp.float32)
    feed_left_out = at.exchange_owners(feed_left.reshape(matrices, row_span, model_width)).astype(
        jnp.float32
    )

    grad_qkv_row, grad_bias = attn_bwd(
        qkv_row,
        grad_attended_row,
        attended_f32,
        log_totals,
        bias_rel,
        seg_col,
        seg_line,
        heads,
        tile,
    )
    grad_qkv = dot(normed_row, grad_qkv_row, 0, 0)
    sum_qkv = at.scatter_parts(grad_qkv.reshape(parts, model_width // parts, 3 * head_width))
    side_rows = model_width // (parts * sides)
    sum_qkv = low(sum_qkv).reshape(sides, side_rows, 3, head_width)
    sum_qkv = jnp.pad(jnp.transpose(sum_qkv, (2, 0, 1, 3)), ((0, 1), (0, 0), (0, 0), (0, 0)))
    sum_qkv = at.exchange(sum_qkv.reshape(seq_size, side_rows, head_width)).reshape(
        micro_rows, at.head_groups, at.repeat, side_rows, head_width
    )
    sum_qkv = jnp.sum(sum_qkv.astype(jnp.float32), axis=(0, 2))
    sum_qkv = at.sum_groups(jnp.transpose(sum_qkv, (1, 0, 2)).reshape(side_rows, model_width))
    full_qkv = at.gather_members(low(sum_qkv)).reshape(model_width, model_width)
    grad_normed_part = low(dot(grad_qkv_row, weights_qkv, 1, 1))
    grad_normed = at.exchange(grad_normed_part.reshape(seq_size, tok_local, model_width))
    grad_normed = jnp.sum(
        grad_normed.reshape(micro_rows, -1, tok_local, model_width).astype(jnp.float32), axis=1
    ).reshape(micro_rows * tok_local, model_width)
    grad_tokens_norm, grad_gain_one = norm_back(tokens, factor_one, vectors[5], grad_normed)
    grad_tokens = (grad_resid + grad_tokens_norm).reshape(micro_rows, tok_local, model_width)

    grad_blend = jnp.repeat(grad_tokens, 2, axis=1) * 0.5
    grad_weights = jnp.stack([jnp.sum(grad_blend * pooled_item, axis=-1) for pooled_item in pooled])
    grad_sizes = size_weights * (
        grad_weights - jnp.sum(size_weights * grad_weights, axis=0, keepdims=True)
    )
    grad_score = sum(
        (
            jnp.sum(grad_sizes[size_index][:, :, None] * pooled[size_index], axis=(0, 1))
            for size_index in range(4)
        )
    )
    grad_pooled = jnp.stack(
        [
            size_weights[size_index][:, :, None] * grad_blend
            + grad_sizes[size_index][:, :, None] * vectors[4]
            for size_index in range(4)
        ]
    )
    wide_grads = padded_2(low(grad_pooled), (("seq", 2),), 6).astype(jnp.float32)
    ext_positions = sequence_position * width_bytes + jnp.arange(width_bytes + 3, dtype=jnp.int32)
    in_range = (ext_positions < row_len).astype(jnp.float32)[:, None]
    grad_conv = jnp.zeros((micro_rows, width_bytes + 3, model_width), jnp.float32)
    for block_size in range(1, 5):
        summed, counted = block_pool(
            wide_grads[block_size - 1][:, 3:], ext_positions, block_size, row_len
        )
        grad_conv = grad_conv + summed / jnp.maximum(counted, 1.0)[:, None] * in_range
    grad_embedded = sum(
        (
            vectors[tap_index] * grad_conv[:, 3 - tap_index : 3 - tap_index + width_bytes]
            for tap_index in range(4)
        )
    )
    grad_taps = [
        jnp.sum(
            grad_conv[:, :width_bytes] * widened[:, 3 + tap_index : 3 + tap_index + width_bytes],
            axis=(0, 1),
        )
        for tap_index in range(4)
    ]
    input_grads = jnp.where(is_valid[:, :, None], grad_embedded, 0.0)
    grad_vectors = jnp.stack(grad_taps + [grad_score, grad_gain_one, grad_gain_two])
    part_grad = jnp.einsum("xb,hx->bh", onehot, grad_bias[:, :-1], precision=HIGH_PRECISION)
    grad_table = lax.dynamic_update_slice_in_dim(
        jnp.zeros_like(bias_table), part_grad, head_begin, 1
    )
    small = jnp.pad(grad_table.reshape(-1), (0, model_width - grad_table.size))
    small = at.sum_all(jnp.concatenate([grad_vectors, small[None]], axis=0))
    sum_vectors = small[:-1]
    sum_table = small[-1, : grad_table.size].reshape(grad_table.shape)
    total_tokens = micro_rows * at.dp_size * tok_row
    small_rate = SMALL_RATE / math.sqrt(total_tokens)
    vector_momenta_new = MOMENTUM * vector_momenta + sum_vectors
    vectors_new = vectors - small_rate * vector_momenta_new
    table_momenta_new = MOMENTUM * table_momenta + sum_table
    table_new = bias_table - small_rate * table_momenta_new

    full_attention = jnp.where(at.matrix == 3, full_output, full_qkv)
    full_attention_t = full_attention.T
    rows = strips(full_attention)
    attention_product = low(
        dot(attention_left_rows, new_momenta(attention_old, full_attention), 1, 0)
    )
    attention_parts = [
        low(dot(rows, full_attention, 1, 1)),
        low(dot(strips(full_attention_t), full_attention_t, 1, 1)),
        low(dot(attention_product, attention_right_whole, 1, 0)),
        rows,
    ]
    attention_out = at.exchange_owners(
        jnp.concatenate(
            [item.reshape(matrices, row_span, model_width) for item in attention_parts], axis=1
        )
    ).astype(jnp.float32)
    sum_left, sum_right, step, grads = [
        attention_out[:, i * row_span : (i + 1) * row_span] for i in range(4)
    ]

    def statistics(old, increment):
        return STAT_DECAY * old + (1.0 - STAT_DECAY) * increment

    attention_new = attention_weights - MATRIX_RATE * step
    attention_left_new = statistics(attention_left, sum_left)
    attention_right_new = statistics(attention_right, sum_right)
    attention_mom_new = MOMENTUM * attention_momenta + grads

    step, grads, sum_right = (
        feed_out[:, :row_span],
        feed_out[:, row_span : 2 * row_span],
        feed_out[:, 2 * row_span :],
    )
    expand_new = expand_weights - MATRIX_RATE * step[:2]
    expand_left_new = statistics(expand_left, feed_left_out[:2])
    expand_right_new = statistics(expand_right, sum_right[:2])
    expand_mom_new = MOMENTUM * expand_momenta + grads[:2]
    shrink_new = shrink_weights - MATRIX_RATE * step[2].reshape(shrink_weights.shape)
    shrink_left_new = statistics(down_left_statistics, sum_right[2])
    shrink_right_new = statistics(shrink_right, feed_left_out[2])
    shrink_mom_new = MOMENTUM * shrink_momenta + grads[2].reshape(shrink_weights.shape)
    return (
        layer_output,
        input_grads,
        vectors_new,
        vector_momenta_new,
        table_new,
        table_momenta_new,
        attention_new,
        attention_left_new,
        attention_right_new,
        attention_mom_new,
        low(attention_new),
        expand_new,
        expand_left_new,
        expand_right_new,
        expand_mom_new,
        low(expand_new),
        shrink_new,
        shrink_left_new,
        shrink_right_new,
        shrink_mom_new,
        low(shrink_new),
    )


def solution(mesh):
    row = P("dp", "seq", None)
    stack = P(None, BOTH, None)
    flat = P(BOTH, None)
    return jax.shard_map(
        per_device,
        mesh=mesh,
        in_specs=(row, P("dp", "seq"), P("dp"), P(), row)
        + (P(),) * 4
        + (stack,) * 12
        + (flat,) * 6,
        out_specs=(row, row) + (P(),) * 4 + (stack,) * 10 + (flat,) * 5,
        check_vma=False,
    )
```

time: 2020 us -> 683 us (0.34)
  waiting for transfers between devices: 1120 us -> 196 us
  local copies, waits for them, and re-layouts: 439 us -> 174 us
  matrix products: 210 us -> 54.9 us
  starting transfers between devices: 14 us -> 108 us
  blocking collectives: 63.5 us -> 0 us
  loops' own time: 46.3 us -> 0 us
  Pallas kernels: 0 us -> 28.8 us
    all_gather x16 -> x4, waiting for transfers between devices: 541 us -> 0.02 us  [the longest x1 0.02 us: gather_holders(): whole = lax.all_gather(block, BOTH, axis=0, axis_index_groups=self.holders)]
    reduce_scatter x3 -> x0, waiting for transfers between devices: 388 us -> none  [the longest x1 158 us: per_device(): lax.psum_scatter(jnp.stack([grad_gate_w, grad_up_w]), ('dp', 'seq'), scat...]
    unnamed x27 -> x4, waiting for transfers between devices: 190 us -> 0.07 us
    dot_general x63 -> x21, matrix products: 210 us -> 54.9 us  [the longest x19 52.5 us: dot(): lax.dot_general(left_side, right_side, (((left_dim,), (right_dim,)), ((),...]
    while x120 -> x0, local copies, waits for them, and re-layouts: 104 us -> none
    ppermute x0 -> x25, waiting for transfers between devices: none -> 99.8 us  [flip(): return lax.ppermute(block, axis, [(i, i ^ bits) for i in range(size)])]
    all_to_all x0 -> x14, waiting for transfers between devices: none -> 95.4 us  [the longest x8 87.7 us: exchange(): return lax.all_to_all(blocks, 'seq', 0, 0, tiled=True)]
    slice x63 -> x5, local copies, waits for them, and re-layouts: 87.9 us -> 5.24 us  [the longest x1 4.24 us: per_device(): feed_old = early[:, 2 * model_width:2 * model_width + hidden_width]]
  transfers between devices with their start and end apart: 27 -> 47, of which waited for: 19 -> 23; matrix products, arithmetic and copies ran while one was open for 28% -> 42% of each run, Pallas kernels for 0% -> 4%
where the time goes in v1:
time: 683 us; the launch traced here: 670 us
  waiting for transfers between devices  196 us (29%)
  local copies, waits for them, and re-layouts  174 us (25%)
  starting transfers between devices  108 us (16%)
  other arithmetic  91.4 us (13%)
  matrix products  54.9 us (8%)
  Pallas kernels  28.8 us (4%)
  between operations  16.3 us (2%)
    ppermute x25, waiting for transfers between devices, flip(): return lax.ppermute(block, axis, [(i, i ^ bits) for i in range(size)])  99.8 us
    all_to_all x8, waiting for transfers between devices, exchange(): return lax.all_to_all(blocks, 'seq', 0, 0, tiled=True)  87.7 us
    dot_general x19, matrix products, dot(): lax.dot_general(left_side, right_side, (((left_dim,), (right_dim,)), ((),...  52.5 us
    all_to_all x8, starting transfers between devices, exchange(): return lax.all_to_all(blocks, 'seq', 0, 0, tiled=True)  39.8 us
    unnamed x237, local copies, waits for them, and re-layouts  26.2 us
    all_to_all x5, starting transfers between devices, exchange_owners(): lax.all_to_all(blocks, 'seq', 0, 0, tiled=True, axis_index_groups=self.ow...  25.8 us
    ppermute x25, starting transfers between devices, flip(): return lax.ppermute(block, axis, [(i, i ^ bits) for i in range(size)])  24.2 us
    pallas_call x1, Pallas kernels, attn_bwd(): pl.pallas_call(functools.partial(attn_bwd_kernel, heads, tile, trans), gr...  19 us
  transfers between devices with their start and end apart: 47, of which 23 were waited for; matrix products, arithmetic and copies ran while one was open for 42% of the time, Pallas kernels for 4%

profile of v1, /device:TPU:0, one launch (start us, length us, event | category | flops | bytes accessed | tf_op | source)
XLA Modules:
  0.0 669.9 jit_solution(15819922328903728764)
XLA Ops:
  12.1 5.5 collective-permute-start
  18.4 6.2 all-to-all-start.2
  31.3 4.7 multiply_reduce_fusion.11
  36.7 6.0 all-to-all-start.1
  42.7 15.2 %all-to-all-done.1 = bf16[8,24,576]{2,1,0:T(8,128)(2,1)S(1)} async-done(((bf16[8,24,576]{2,1,0:T(8,128)(2,1)}), bf16[8,24,576]{2,1,0:T(8,128)(2,1)S(1)}, u32[]{:S(2)}, u32[]{:S(2)}) %all-to-all-start.1) | async-done | bytes 221216 | tf_op jit(solution)/shard_map/all_to_all | solution.py:304
  73.3 25.3 %all-to-all-done.7 = bf16[8,24,2176]{2,1,0:T(8,128)(2,1)} async-done(((bf16[8,24,2176]{2,1,0:T(8,128)(2,1)}), bf16[8,24,2176]{2,1,0:T(8,128)(2,1)}, u32[]{:S(2)}, u32[]{:S(2)}) %all-to-all-start.7) | async-done | bytes 835616 | tf_op jit(solution)/shard_map/all_to_all | solution.py:304
  121.0 23.8 %all-to-all-done = bf16[8,128,768]{1,2,0:T(8,128)(2,1)} async-done(((bf16[8,128,768]{1,2,0:T(8,128)(2,1)}), bf16[8,128,768]{1,2,0:T(8,128)(2,1)}, u32[]{:S(2)}, u32[]{:S(2)}) %all-to-all-start) | async-done | bytes 1572896 | tf_op jit(solution)/shard_map/all_to_all | solution.py:304
  150.3 9.8 %shard_map.418 = (bf16[1024,192]{1,0:T(8,128)(2,1)S(1)}, f32[1024,192]{1,0:T(8,128)S(1)}, f32[1024,128]{1,0:T(8,128)S(1)}) custom-call(bf16[1024,576]{1,0:T(8,128)(2,1)S(1)} %convolution_convert_fusion.2.qkv_ref, f32[3,2048]{1,0:T(4,128)S(1)} %pad.16.brel_ref, s32[1024,1]{1,0:T(8,128)S(1)} %copy.219.segc_ref, s32[1,1024]{1,0:T(1,128)S(1)} %bitcast.334), custom_call_target="tpu_custom_call" | custom-call | flops 805306368 | bytes 2359296 | tf_op jit(solution)/shard_map/pallas_call | solution.py:72
  210.6 9.6 %collective-permute-done.14 = bf16[1,256,768]{2,1,0:T(8,128)(2,1)S(1)} collective-permute-done((bf16[1,256,768]{2,1,0:T(8,128)(2,1)S(1)}, bf16[1,256,768]{2,1,0:T(8,128)(2,1)S(1)}, u32[]{:S(2)}, u32[]{:S(2)}) %collective-permute-start.14) | collective-permute-done | bytes 393248 | tf_op jit(solution)/shard_map/ppermute | solution.py:253
  220.6 7.4 %collective-permute-done.9 = bf16[1,256,768]{2,1,0:T(8,128)(2,1)S(1)} collective-permute-done((bf16[1,256,768]{2,1,0:T(8,128)(2,1)S(1)}, bf16[1,256,768]{2,1,0:T(8,128)(2,1)S(1)}, u32[]{:S(2)}, u32[]{:S(2)}) %collective-permute-start.9) | collective-permute-done | bytes 393248 | tf_op jit(solution)/shard_map/ppermute | solution.py:253
  240.9 6.1 all-to-all-start.4
  254.5 4.9 all-to-all-done.4
  261.4 19.0 %shard_map.419 = (bf16[1024,576]{1,0:T(8,128)(2,1)}, f32[3,2048]{1,0:T(4,128)}) custom-call(bf16[1024,576]{1,0:T(8,128)(2,1)} %copy-done.3, bf16[1024,192]{1,0:T(8,128)(2,1)} %bitcast.406, f32[1024,192]{1,0:T(8,128)} %copy-done.4, f32[1024,128]{1,0:T(8,128)} %copy-done.5, f32[3,2048]{1,0:T(4,128)} %copy-done.1, s32[1024,1]{1,0:T(8,128)} %copy-done, ...), custom_call_target="tpu_custom_call" | custom-call | flops 2013265920 | bytes 4718592 | tf_op jit(solution)/shard_map/pallas_call | solution.py:147
  296.8 6.2 collective-permute-done.28
  318.4 14.1 %all-to-all-done.6 = bf16[8,96,192]{2,1,0:T(8,128)(2,1)} async-done(((bf16[8,96,192]{2,1,0:T(8,128)(2,1)}), bf16[8,96,192]{2,1,0:T(8,128)(2,1)}, u32[]{:S(2)}, u32[]{:S(2)}) %all-to-all-start.6) | async-done | bytes 294944 | tf_op jit(solution)/shard_map/all_to_all | solution.py:304
  354.3 26.5 %collective-permute-done.25 = bf16[2,384,512]{2,1,0:T(8,128)(2,1)} collective-permute-done((bf16[2,384,512]{2,1,0:T(8,128)(2,1)}, bf16[2,384,512]{2,1,0:T(8,128)(2,1)}, u32[]{:S(2)}, u32[]{:S(2)}) %collective-permute-start.25) | collective-permute-done | bytes 786464 | tf_op jit(solution)/shard_map/ppermute | solution.py:253
  385.4 16.1 %collective-permute-done.26 = bf16[1,384,512]{2,1,0:T(8,128)(2,1)S(1)} collective-permute-done((bf16[1,384,512]{2,1,0:T(8,128)(2,1)S(1)}, bf16[1,384,512]{2,1,0:T(8,128)(2,1)S(1)}, u32[]{:S(2)}, u32[]{:S(2)}) %collective-permute-start.26) | collective-permute-done | bytes 393248 | tf_op jit(solution)/shard_map/ppermute | solution.py:253
  404.6 12.6 %copy.240 = bf16[4,192,2,2176]{3,2,1,0:T(2,128)(2,1)S(1)} copy(bf16[4,192,2,2176]{3,1,2,0:T(8,128)(2,1)} %bitcast.352) | data formatting | bytes 13369344 | tf_op jit(solution)/shard_map/transpose | solution.py:443
  425.4 6.6 reshape.1229
  432.0 4.7 copy.241
  472.1 7.0 %all-to-all-start.10 = ((bf16[4,64,2048]{2,1,0:T(8,128)(2,1)}), bf16[4,64,2048]{2,1,0:T(8,128)(2,1)}, u32[]{:S(2)}, u32[]{:S(2)}) async-start(bf16[4,64,2048]{2,1,0:T(8,128)(2,1)} %maximum_maximum_fusion), calls=%async_computation.10 | async-start | bytes 2097152 | tf_op jit(solution)/shard_map/all_to_all | solution.py:320
  479.1 5.5 slice_bitcast_fusion.3
  505.0 6.0 copy.242
  511.0 6.1 reshape_reshape.25
  521.8 4.6 copy.247
  535.4 7.2 %convolution_convert_fusion.6 = bf16[768,256]{1,0:T(8,128)(2,1)} fusion(bf16[768,4352]{1,0:T(8,128)(2,1)} %bitcast.345, bf16[256,2048]{1,0:T(8,128)(2,1)} %bitcast.127, bf16[768,2048]{1,0:T(8,128)(2,1)} %bitcast.337, bf16[2048,768]{0,1:T(8,128)(2,1)} %copy.241, pred[]{:T(512)S(6)} %eq.311), kind=kOutput, calls=%fused_computation.138 | convolution fusion | flops 1117126656 | bytes 12058625 | tf_op jit(solution)/shard_map/dot_general | solution.py:164
  549.8 5.1 all-to-all-start.13
  568.1 5.1 all-to-all-done.11
  598.0 5.1 all-to-all-start.12
  603.3 6.1 fusion.22
  623.1 10.1 %collective-permute-done.20 = f32[8,768]{1,0:T(8,128)S(1)} collective-permute-done((f32[8,768]{1,0:T(8,128)S(1)}, f32[8,768]{1,0:T(8,128)S(1)}, u32[]{:S(2)}, u32[]{:S(2)}) %collective-permute-start.20) | collective-permute-done | bytes 24608 | tf_op jit(solution)/shard_map/ppermute | solution.py:253
  638.0 8.6 %collective-permute-done.21 = f32[8,768]{1,0:T(8,128)S(1)} collective-permute-done((f32[8,768]{1,0:T(8,128)S(1)}, f32[8,768]{1,0:T(8,128)S(1)}, u32[]{:S(2)}, u32[]{:S(2)}) %collective-permute-start.21) | collective-permute-done | bytes 24608 | tf_op jit(solution)/shard_map/ppermute | solution.py:253
  (556 shorter events, 346.6 us)
Async XLA Ops:
  7.2 173.8 %all-gather.5.cloned.1.call-start = ((), (), s32[]{:S(2)}) async-start(), calls=%async_computation.14 | async-start | bytes 10948608 | tf_op jit(solution)/shard_map/all_gather | solution.py:332
  10.6 19.2 %collective-permute-start.1 = (bf16[2,6,768]{2,1,0:T(8,128)(2,1)S(1)}, bf16[2,6,768]{2,1,0:T(8,128)(2,1)S(1)}, u32[]{:S(2)}, u32[]{:S(2)}) collective-permute-start(bf16[2,6,768]{2,1,0:T(8,128)(2,1)S(1)} %get-tuple-element.226), channel_id=1, source_target_pairs={{1,0},{2,1},{3,2},{4,3},{5,4},{6,5},{7,6},{9,8},{10,9},{11,10},{12... | collective-permute-start | bytes 55304 | tf_op jit(solution)/shard_map/ppermute | solution.py:180
  12.1 17.8 %collective-permute-start = (bf16[2,6,768]{2,1,0:T(8,128)(2,1)S(1)}, bf16[2,6,768]{2,1,0:T(8,128)(2,1)S(1)}, u32[]{:S(2)}, u32[]{:S(2)}) collective-permute-start(bf16[2,6,768]{2,1,0:T(8,128)(2,1)S(1)} %get-tuple-element.225), channel_id=1, source_target_pairs={{0,1},{1,2},{2,3},{3,4},{4,5},{5,6},{6,7},{8,9},{9,10},{10,11},{11... | collective-permute-start | bytes 55304 | tf_op jit(solution)/shard_map/ppermute | solution.py:177
  18.4 17.6 %all-to-all-start.2 = ((s32[8,1,128]{2,1,0:T(1,128)}), s32[8,1,128]{2,1,0:T(1,128)S(1)}, u32[]{:S(2)}, u32[]{:S(2)}) async-start(s32[8,1,128]{2,1,0:T(1,128)} %bitcast.20), calls=%async_computation.2 | async-start | bytes 8192 | tf_op jit(solution)/shard_map/all_to_all | solution.py:304
  36.7 21.3 %all-to-all-start.1 = ((bf16[8,24,576]{2,1,0:T(8,128)(2,1)}), bf16[8,24,576]{2,1,0:T(8,128)(2,1)S(1)}, u32[]{:S(2)}, u32[]{:S(2)}) async-start(bf16[8,24,576]{2,1,0:T(8,128)(2,1)} %bitcast.393), calls=%async_computation.1 | async-start | bytes 491520 | tf_op jit(solution)/shard_map/all_to_all | solution.py:304
  58.0 40.7 %all-to-all-start.7 = ((bf16[8,24,2176]{2,1,0:T(8,128)(2,1)}), bf16[8,24,2176]{2,1,0:T(8,128)(2,1)}, u32[]{:S(2)}, u32[]{:S(2)}) async-start(bf16[8,24,2176]{2,1,0:T(8,128)(2,1)} %copy.239), calls=%async_computation.7 | async-start | bytes 1671168 | tf_op jit(solution)/shard_map/all_to_all | solution.py:304
  100.1 44.8 %all-to-all-start = ((bf16[8,128,768]{1,2,0:T(8,128)(2,1)}), bf16[8,128,768]{1,2,0:T(8,128)(2,1)}, u32[]{:S(2)}, u32[]{:S(2)}) async-start(bf16[8,128,768]{1,2,0:T(8,128)(2,1)} %bitcast.355), calls=%async_computation | async-start | bytes 3145728 | tf_op jit(solution)/shard_map/all_to_all | solution.py:304
  104.5 300.1 %all-gather.11.cloned.1.call-start = ((), (), s32[]{:S(2)}) async-start(), calls=%async_computation.17 | async-start | bytes 7520256 | tf_op jit(solution)/shard_map/all_gather | solution.py:311
  106.3 62.8 %collective-permute-start.11 = (bf16[256,768]{1,0:T(8,128)(2,1)}, bf16[256,768]{1,0:T(8,128)(2,1)}, u32[]{:S(2)}, u32[]{:S(2)}) collective-permute-start(bf16[256,768]{1,0:T(8,128)(2,1)} %bitcast.40), channel_id=1, source_target_pairs={{0,8},{8,0},{16,24},{24,16},{1,9},{9,1},{17,25},{25,17},{2,10},{10... | collective-permute-start | bytes 1179656 | tf_op jit(solution)/shard_map/ppermute | solution.py:253
  107.9 10.3 %collective-permute-start.2 = (bf16[192,576]{1,0:T(8,128)(2,1)S(1)}, bf16[192,576]{1,0:T(8,128)(2,1)}, u32[]{:S(2)}, u32[]{:S(2)}) collective-permute-start(bf16[192,576]{1,0:T(8,128)(2,1)S(1)} %bitcast.390), channel_id=1, source_target_pairs={{0,16},{8,24},{16,0},{24,8},{1,17},{9,25},{17,1},{25,9},{2,18},{10... | collective-permute-start | bytes 663560 | tf_op jit(solution)/shard_map/ppermute | solution.py:253
  114.6 56.3 %collective-permute-start.12 = (bf16[256,768]{1,0:T(8,128)(2,1)}, bf16[256,768]{1,0:T(8,128)(2,1)}, u32[]{:S(2)}, u32[]{:S(2)}) collective-permute-start(bf16[256,768]{1,0:T(8,128)(2,1)} %collective-permute-done.10), channel_id=1, source_target_pairs={{0,8},{8,0},{16,24},{24,16},{1,9},{9,1},{17,25},{25,17},{2,10},{10... | collective-permute-start | bytes 1179656 | tf_op jit(solution)/shard_map/ppermute | solution.py:253
  162.8 15.8 %all-to-all-start.3 = ((bf16[8,128,192]{1,2,0:T(8,128)(2,1)}), bf16[8,128,192]{1,2,0:T(8,128)(2,1)}, u32[]{:S(2)}, u32[]{:S(2)}) async-start(bf16[8,128,192]{1,2,0:T(8,128)(2,1)} %copy.220), calls=%async_computation.3 | async-start | bytes 786432 | tf_op jit(solution)/shard_map/all_to_all | solution.py:304
  208.2 12.0 %collective-permute-start.14 = (bf16[1,256,768]{2,1,0:T(8,128)(2,1)S(1)}, bf16[1,256,768]{2,1,0:T(8,128)(2,1)S(1)}, u32[]{:S(2)}, u32[]{:S(2)}) collective-permute-start(bf16[1,256,768]{2,1,0:T(8,128)(2,1)S(1)} %dynamic-slice_convert_fusion.4), channel_id=1, source_target_pairs={{0,16},{8,24},{16,0},{24,8},{1,17},{9,25},{17,1},{25,9},{2,18},{10... | collective-permute-start | bytes 1179656 | tf_op jit(solution)/shard_map/ppermute | solution.py:253
  210.0 18.0 %collective-permute-start.9 = (bf16[1,256,768]{2,1,0:T(8,128)(2,1)S(1)}, bf16[1,256,768]{2,1,0:T(8,128)(2,1)S(1)}, u32[]{:S(2)}, u32[]{:S(2)}) collective-permute-start(bf16[1,256,768]{2,1,0:T(8,128)(2,1)S(1)} %dynamic-slice_convert_fusion.5), channel_id=1, source_target_pairs={{0,16},{8,24},{16,0},{24,8},{1,17},{9,25},{17,1},{25,9},{2,18},{10... | collective-permute-start | bytes 1179656 | tf_op jit(solution)/shard_map/ppermute | solution.py:253
  232.8 17.9 %collective-permute-start.22 = (bf16[2,192,768]{2,1,0:T(8,128)(2,1)}, bf16[2,192,768]{2,1,0:T(8,128)(2,1)}, u32[]{:S(2)}, u32[]{:S(2)}) collective-permute-start(bf16[2,192,768]{2,1,0:T(8,128)(2,1)} %fusion.84), channel_id=1, source_target_pairs={{0,8},{8,0},{16,24},{24,16},{1,9},{9,1},{17,25},{25,17},{2,10},{10... | collective-permute-start | bytes 1769480 | tf_op jit(solution)/shard_map/ppermute | solution.py:253
  240.9 18.5 %all-to-all-start.4 = ((bf16[8,128,192]{1,2,0:T(8,128)(2,1)}), bf16[8,128,192]{1,2,0:T(8,128)(2,1)}, u32[]{:S(2)}, u32[]{:S(2)}) async-start(bf16[8,128,192]{1,2,0:T(8,128)(2,1)} %bitcast.376), calls=%async_computation.4 | async-start | bytes 786432 | tf_op jit(solution)/shard_map/all_to_all | solution.py:304
  253.0 31.2 %collective-permute-start.23 = (bf16[1,192,768]{2,1,0:T(8,128)(2,1)S(1)}, bf16[1,192,768]{2,1,0:T(8,128)(2,1)}, u32[]{:S(2)}, u32[]{:S(2)}) collective-permute-start(bf16[1,192,768]{2,1,0:T(8,128)(2,1)S(1)} %dynamic-slice_convert_fusion.6), channel_id=1, source_target_pairs={{0,16},{8,24},{16,0},{24,8},{1,17},{9,25},{17,1},{25,9},{2,18},{10... | collective-permute-start | bytes 884744 | tf_op jit(solution)/shard_map/ppermute | solution.py:253
  291.7 49.4 %collective-permute-start.24 = (bf16[4,384,512]{2,1,0:T(8,128)(2,1)}, bf16[4,384,512]{2,1,0:T(8,128)(2,1)}, u32[]{:S(2)}, u32[]{:S(2)}) collective-permute-start(bf16[4,384,512]{2,1,0:T(8,128)(2,1)} %dynamic-slice_bitcast_fusion), channel_id=1, source_target_pairs={{0,1},{1,0},{2,3},{3,2},{4,5},{5,4},{6,7},{7,6},{8,9},{9,8},{10,11... | collective-permute-start | bytes 4718600 | tf_op jit(solution)/shard_map/ppermute | solution.py:253
  308.8 23.7 %all-to-all-start.6 = ((bf16[8,96,192]{2,1,0:T(8,128)(2,1)}), bf16[8,96,192]{2,1,0:T(8,128)(2,1)}, u32[]{:S(2)}, u32[]{:S(2)}) async-start(bf16[8,96,192]{2,1,0:T(8,128)(2,1)} %bitcast.377), calls=%async_computation.6 | async-start | bytes 786432 | tf_op jit(solution)/shard_map/all_to_all | solution.py:304
  332.5 105.6 %all-to-all-start.5 = ((bf16[8,128,768]{2,1,0:T(8,128)(2,1)}), bf16[8,128,768]{2,1,0:T(8,128)(2,1)}, u32[]{:S(2)}, u32[]{:S(2)}) async-start(bf16[8,128,768]{2,1,0:T(8,128)(2,1)} %bitcast.364), calls=%async_computation.5 | async-start | bytes 3145728 | tf_op jit(solution)/shard_map/all_to_all | solution.py:304
  336.8 147.8 %all-gather.9.cloned.1.call-start = ((), (), s32[]{:S(2)}) async-start(), calls=%async_computation.16 | async-start | bytes 1327104 | tf_op jit(solution)/shard_map/all_gather | solution.py:307
  341.0 146.7 %all-gather.7.cloned.1.call-start = ((), (), s32[]{:S(2)}) async-start(), calls=%async_computation.15 | async-start | bytes 3538944 | tf_op jit(solution)/shard_map/all_gather | solution.py:307
  346.1 34.8 %collective-permute-start.25 = (bf16[2,384,512]{2,1,0:T(8,128)(2,1)}, bf16[2,384,512]{2,1,0:T(8,128)(2,1)}, u32[]{:S(2)}, u32[]{:S(2)}) collective-permute-start(bf16[2,384,512]{2,1,0:T(8,128)(2,1)} %fusion.74), channel_id=1, source_target_pairs={{0,2},{1,3},{2,0},{3,1},{4,6},{5,7},{6,4},{7,5},{8,10},{9,11},{10,... | collective-permute-start | bytes 2359304 | tf_op jit(solution)/shard_map/ppermute | solution.py:253
  382.8 18.7 %collective-permute-start.26 = (bf16[1,384,512]{2,1,0:T(8,128)(2,1)S(1)}, bf16[1,384,512]{2,1,0:T(8,128)(2,1)S(1)}, u32[]{:S(2)}, u32[]{:S(2)}) collective-permute-start(bf16[1,384,512]{2,1,0:T(8,128)(2,1)S(1)} %dynamic-slice_convert_fusion.3), channel_id=1, source_target_pairs={{0,4},{1,5},{2,6},{3,7},{4,0},{5,1},{6,2},{7,3},{8,12},{9,13},{10,... | collective-permute-start | bytes 1179656 | tf_op jit(solution)/shard_map/ppermute | solution.py:253
  438.1 34.0 %all-to-all-start.8 = ((bf16[4,24,768]{2,1,0:T(8,128)(2,1)}), bf16[4,24,768]{2,1,0:T(8,128)(2,1)S(1)}, u32[]{:S(2)}, u32[]{:S(2)}) async-start(bf16[4,24,768]{2,1,0:T(8,128)(2,1)} %convert_element_type.755), calls=%async_computation.8 | async-start | bytes 294912 | tf_op jit(solution)/shard_map/all_to_all | solution.py:320
  472.1 63.3 %all-to-all-start.10 = ((bf16[4,64,2048]{2,1,0:T(8,128)(2,1)}), bf16[4,64,2048]{2,1,0:T(8,128)(2,1)}, u32[]{:S(2)}, u32[]{:S(2)}) async-start(bf16[4,64,2048]{2,1,0:T(8,128)(2,1)} %maximum_maximum_fusion), calls=%async_computation.10 | async-start | bytes 2097152 | tf_op jit(solution)/shard_map/all_to_all | solution.py:320
  549.8 11.2 %all-to-all-start.13 = ((bf16[4,24,768]{2,1,0:T(8,128)(2,1)}), bf16[4,24,768]{2,1,0:T(8,128)(2,1)}, u32[]{:S(2)}, u32[]{:S(2)}) async-start(bf16[4,24,768]{2,1,0:T(8,128)(2,1)} %bitcast.141), calls=%async_computation.13 | async-start | bytes 294912 | tf_op jit(solution)/shard_map/all_to_all | solution.py:320
  561.0 12.2 %all-to-all-start.11 = ((bf16[8,96,256]{2,1,0:T(8,128)(2,1)}), bf16[8,96,256]{2,1,0:T(8,128)(2,1)}, u32[]{:S(2)}, u32[]{:S(2)}) async-start(bf16[8,96,256]{2,1,0:T(8,128)(2,1)} %bitcast.375), calls=%async_computation.11 | async-start | bytes 786432 | tf_op jit(solution)/shard_map/all_to_all | solution.py:315
  573.1 24.9 %all-to-all-start.9 = ((bf16[4,96,768]{2,1,0:T(8,128)(2,1)}), bf16[4,96,768]{2,1,0:T(8,128)(2,1)}, u32[]{:S(2)}, u32[]{:S(2)}) async-start(bf16[4,96,768]{2,1,0:T(8,128)(2,1)} %pad_maximum_fusion.5), calls=%async_computation.9 | async-start | bytes 1179648 | tf_op jit(solution)/shard_map/all_to_all | solution.py:320
  598.0 55.4 %all-to-all-start.12 = ((bf16[4,112,2048]{2,1,0:T(8,128)(2,1)}), bf16[4,112,2048]{2,1,0:T(8,128)(2,1)}, u32[]{:S(2)}, u32[]{:S(2)}) async-start(bf16[4,112,2048]{2,1,0:T(8,128)(2,1)} %pad_maximum_fusion), calls=%async_computation.12 | async-start | bytes 3670016 | tf_op jit(solution)/shard_map/all_to_all | solution.py:320
  621.0 12.1 %collective-permute-start.20 = (f32[8,768]{1,0:T(8,128)S(1)}, f32[8,768]{1,0:T(8,128)S(1)}, u32[]{:S(2)}, u32[]{:S(2)}) collective-permute-start(f32[8,768]{1,0:T(8,128)S(1)} %add.1405), channel_id=1, source_target_pairs={{0,2},{1,3},{2,0},{3,1},{4,6},{5,7},{6,4},{7,5},{8,10},{9,11},{10,... | collective-permute-start | bytes 73736 | tf_op jit(solution)/shard_map/ppermute | solution.py:253
  633.2 13.4 %collective-permute-start.21 = (f32[8,768]{1,0:T(8,128)S(1)}, f32[8,768]{1,0:T(8,128)S(1)}, u32[]{:S(2)}, u32[]{:S(2)}) collective-permute-start(f32[8,768]{1,0:T(8,128)S(1)} %add.1406), channel_id=1, source_target_pairs={{0,4},{1,5},{2,6},{3,7},{4,0},{5,1},{6,2},{7,3},{8,12},{9,13},{10,... | collective-permute-start | bytes 73736 | tf_op jit(solution)/shard_map/ppermute | solution.py:253
  (129 other events, 1133.7 us)
Sparse Core Ops, SparseCore 0:
  11.6 109.5 all-gather.4
  123.1 56.7 all-gather.10
  341.1 30.4 all-gather.8
  402.5 32.2 all-gather.6
